TPU v7x, 32 devices: a whole 2x2x4 slice. The times are simulated.
32 devices in a mesh: segment: 2 (over y), seq: 4 (over x, core), tp: 4 (over z).
Axes of the slice: x: 2, y: 2, z: 4, core: 2. Of those that a mesh axis runs over, the one named last changes fastest.
Arguments:
- queries: bfloat16 [2, 768, 4096], P('segment', 'seq', 'tp'), may hold values from -64 to 64
- nb_keys: bfloat16 [2, 12, 256, 4096], P('segment', 'seq', None, 'tp'), may hold values from -24 to 24
- nb_values: bfloat16 [2, 12, 256, 4096], P('segment', 'seq', None, 'tp'), may hold values from -6 to 6
- nb_lengths: int32 [2, 12, 2], P('segment', 'seq'), may hold values from 1 to 128
- slot_stretch: int32 [2, 12], P('segment', 'seq'), may hold values from 0 to 11, as said below
- out_weight: bfloat16 [2, 4096, 4096], P('segment', 'tp', 'seq'), may hold values from -0.09375 to 0.09375
- residual: bfloat16 [2, 768, 4096], P('segment', 'seq', 'tp'), may hold values from -6 to 6
Outputs:
- mixed: bfloat16 [2, 768, 4096], P('segment', 'seq', 'tp')
Inputs may be any that keep to these rules, and one draw needn't show every extreme that they name: Each row slot_stretch[e] is a permutation of the 12 stretches. The 3 stretches of one decoder device (stretches i * 3 to i * 3 + 2) are served by slots on 3 different encoder devices, so one decoder device sends at most one stretch to one encoder device.
All inputs are finite; a program needn't handle non-finite values.
Results may differ from a plain program's by a relative error of at most 0.0034.
Values may be sent and summed in bfloat16 or wider, within the bound.
A program may use at most 64 MiB of HBM per device.

v0:
```python
import math

import jax
import jax.numpy as jnp
from jax import lax
from jax.sharding import PartitionSpec as P

HD = 128
STRETCH = 64
NR = 128


def shifted(value, axis, by):
    size = lax.axis_size(axis)
    return lax.ppermute(value, axis, [(i, (i + by) % size) for i in range(size)])


def attend(query_rows, key_rows, value_rows, lengths):
    count, width, feats = query_rows.shape
    heads = feats // HD
    span = key_rows.shape[1]
    query_heads = query_rows.reshape(count, width, heads, HD)
    key_heads = key_rows.reshape(count, span, heads, HD)
    value_heads = value_rows.reshape(count, span, heads, HD)
    scores = jnp.einsum(
        "cqhd,clhd->chql", query_heads, key_heads, preferred_element_type=jnp.float32
    ) * (1.0 / math.sqrt(HD))
    position = jnp.arange(span, dtype=jnp.int32)
    limits = jnp.take(lengths, position // NR, axis=1)
    valid = ((position % NR)[None, :] < limits)[:, None, None, :]
    highest = jnp.max(jnp.where(valid, scores, -1e30), axis=-1, keepdims=True)
    expo = jnp.exp(jnp.where(valid, scores - highest, -1e30))
    weights = (expo / jnp.sum(expo, axis=-1, keepdims=True)).astype(jnp.bfloat16)
    mixed = jnp.einsum("chql,clhd->cqhd", weights, value_heads, preferred_element_type=jnp.float32)
    return mixed.astype(jnp.bfloat16).reshape(count, width, feats)


def holders_for(table_row, owner_index, per_dev):
    wanted = owner_index * per_dev + jnp.arange(per_dev, dtype=jnp.int32)
    slot_ids = jnp.arange(table_row.shape[0], dtype=jnp.int32)
    matched = table_row[None, :] == wanted[:, None]
    return jnp.sum(jnp.where(matched, slot_ids[None, :] // per_dev, 0), axis=1)


def anchors_for(table_row, holder_index, per_dev):
    return lax.dynamic_slice_in_dim(table_row, holder_index * per_dev, per_dev) // per_dev


def place(blocks_in, targets, count_dev):
    selector = (targets[:, None] == jnp.arange(count_dev, dtype=jnp.int32)[None, :]).astype(
        jnp.bfloat16
    )
    return jnp.einsum(
        "kd,kqf->dqf", selector, blocks_in, preferred_element_type=jnp.float32
    ).astype(jnp.bfloat16)


def local(queries, nb_keys, nb_values, nb_lengths, slot_stretch, out_weight, residual):
    count_dev = lax.axis_size("seq")
    seq_index = lax.axis_index("seq")
    per_dev = slot_stretch.shape[1]
    feats = queries.shape[2]
    key_local = nb_keys[0]
    value_local = nb_values[0]
    length_local = nb_lengths[0]
    blocks = queries[0].reshape(per_dev, STRETCH, feats)
    table_row = lax.all_gather(slot_stretch, "seq", axis=1, tiled=True)[0]
    lowered = shifted(blocks, "segment", -1)
    targets = holders_for(table_row, seq_index, per_dev)
    anchors = anchors_for(table_row, seq_index, per_dev)
    outgoing = place(lowered, targets, count_dev)
    picked = jnp.take(
        lax.all_to_all(outgoing, "seq", split_axis=0, concat_axis=0, tiled=True), anchors, axis=0
    )
    answer = attend(picked, key_local, value_local, length_local)
    returned = lax.all_to_all(
        place(answer, anchors, count_dev), "seq", split_axis=0, concat_axis=0, tiled=True
    )
    gathered = jnp.take(returned, targets, axis=0)
    cca_blocks = shifted(gathered, "segment", 1)
    cca_rows = cca_blocks.reshape(per_dev * STRETCH, feats)
    partial_out = jnp.dot(
        cca_rows,
        lax.all_gather(out_weight[0], "seq", axis=1, tiled=True),
        preferred_element_type=jnp.float32,
    )
    summed = lax.psum_scatter(partial_out, "tp", scatter_dimension=1, tiled=True)
    mixed = (residual[0].astype(jnp.float32) + summed).astype(jnp.bfloat16)
    return mixed[None]


def solution(mesh):
    in_specs = (
        P("segment", "seq", "tp"),
        P("segment", "seq", None, "tp"),
        P("segment", "seq", None, "tp"),
        P("segment", "seq", None),
        P("segment", "seq"),
        P("segment", "tp", "seq"),
        P("segment", "seq", "tp"),
    )
    out_specs = P("segment", "seq", "tp")
    return jax.shard_map(local, mesh=mesh, in_specs=in_specs, out_specs=out_specs, check_vma=False)
```

profile of v0, /device:TPU:2, one launch (start us, length us, event | category | flops | bytes accessed | tf_op | source)
XLA Modules:
  0.0 155.9 jit_solution(137096180656540293)
XLA Ops:
  6.6 0.7 all-gather.3.cloned.1.call-update
  7.6 1.1 copy.31
  8.7 1.5 collective-permute-start
  10.2 0.6 dynamic-slice.1
  11.5 0.7 gather_fusion
  12.5 4.3 %all-reduce = s32[12]{0:T(128)S(1)} all-reduce(s32[12]{0:T(128)S(1)} %bitcast_dynamic-update-slice_fusion), channel_id=1, replica_groups=mesh['segment'=2,'seq'=4,'tp'=4] {'seq'}, use_global_device_ids=true, to_apply=%add | all-reduce | flops 12 | bytes 96
  17.3 3.3 %copy.43 = bf16[96,8,8,128]{3,2,1,0:T(8,128)(2,1)} copy(bf16[96,8,8,128]{3,1,2,0:T(8,128)(2,1)} %bitcast.52) | data formatting | bytes 3145728
  20.9 1.8 %collective-permute-done = bf16[3,64,1024]{2,0,1:T(4,128)(2,1)} collective-permute-done((bf16[3,64,1024]{2,0,1:T(4,128)(2,1)}, bf16[3,64,1024]{2,0,1:T(4,128)(2,1)}, u32[]{:S(2)}, u32[]{:S(2)}) %collective-permute-start) | collective-permute-done | bytes 393248 | tf_op jit(solution)/shard_map/ppermute | solution.py:15
  22.7 1.5 convolution_convert_fusion.1
  24.2 0.9 copy.32
  25.1 3.7 %all-to-all-start = ((bf16[4,64,1024]{2,1,0:T(8,128)(2,1)}), bf16[4,64,1024]{2,1,0:T(8,128)(2,1)S(1)}, u32[]{:S(2)}, u32[]{:S(2)}) async-start(bf16[4,64,1024]{2,1,0:T(8,128)(2,1)} %copy.32), calls=%async_computation | async-start | bytes 1048576 | tf_op jit(solution)/shard_map/all_to_all | solution.py:73
  29.0 12.8 %all-to-all-done = bf16[4,64,1024]{2,1,0:T(8,128)(2,1)S(1)} async-done(((bf16[4,64,1024]{2,1,0:T(8,128)(2,1)}), bf16[4,64,1024]{2,1,0:T(8,128)(2,1)S(1)}, u32[]{:S(2)}, u32[]{:S(2)}) %all-to-all-start) | async-done | bytes 524320 | tf_op jit(solution)/shard_map/all_to_all | solution.py:73
  42.3 0.7 fusion.10
  43.1 0.8 fusion.35
  43.9 0.6 copy-done.2
  45.7 1.0 copy.38
  46.7 5.3 %all-to-all-start.1 = ((bf16[4,64,1024]{2,1,0:T(8,128)(2,1)}), bf16[4,64,1024]{2,1,0:T(8,128)(2,1)S(1)}, u32[]{:S(2)}, u32[]{:S(2)}) async-start(bf16[4,64,1024]{2,1,0:T(8,128)(2,1)} %copy.38), calls=%async_computation.1 | async-start | bytes 1048576 | tf_op jit(solution)/shard_map/all_to_all | solution.py:76
  52.1 12.9 %all-to-all-done.1 = bf16[4,64,1024]{2,1,0:T(8,128)(2,1)S(1)} async-done(((bf16[4,64,1024]{2,1,0:T(8,128)(2,1)}), bf16[4,64,1024]{2,1,0:T(8,128)(2,1)S(1)}, u32[]{:S(2)}, u32[]{:S(2)}) %all-to-all-start.1) | async-done | bytes 524320 | tf_op jit(solution)/shard_map/all_to_all | solution.py:76
  65.7 1.9 %collective-permute-start.1 = (bf16[3,64,1024]{2,1,0:T(8,128)(2,1)S(1)}, bf16[3,64,1024]{2,1,0:T(8,128)(2,1)S(1)}, u32[]{:S(2)}, u32[]{:S(2)}) collective-permute-start(bf16[3,64,1024]{2,1,0:T(8,128)(2,1)S(1)} %broadcast_select_fusion), channel_id=1, source_target_pairs={{0,16},{16,0},{1,17},{17,1},{2,18},{18,2},{3,19},{19,3},{4,20},{20... | collective-permute-start | bytes 1179656 | tf_op jit(solution)/shard_map/ppermute | solution.py:15
  67.6 9.3 %collective-permute-done.1 = bf16[3,64,1024]{2,1,0:T(8,128)(2,1)S(1)} collective-permute-done((bf16[3,64,1024]{2,1,0:T(8,128)(2,1)S(1)}, bf16[3,64,1024]{2,1,0:T(8,128)(2,1)S(1)}, u32[]{:S(2)}, u32[]{:S(2)}) %collective-permute-start.1) | collective-permute-done | bytes 393248 | tf_op jit(solution)/shard_map/ppermute | solution.py:15
  76.8 1.7 %all-gather.3.cloned.1.call-done = bf16[1,1024,4096]{2,1,0:T(8,128)(2,1)} async-done(((bf16[1,1024,1024]{2,1,0:T(8,128)(2,1)}), bf16[1,1024,4096]{2,1,0:T(8,128)(2,1)}) %all-gather.3.cloned.1.call-update) | async-done | bytes 8388624 | tf_op jit(solution)/shard_map/all_gather | solution.py:84
  78.6 6.9 %fusion.1 = f32[192,4096]{1,0:T(8,128)} fusion(bf16[192,1024]{1,0:T(8,128)(2,1)S(1)} %bitcast.54, bf16[1,1024,4096]{2,1,0:T(8,128)(2,1)} %all-gather.3.cloned.1.call-done), kind=kOutput, calls=%fused_computation.4 | convolution fusion | flops 1610612736 | bytes 11927552 | tf_op jit(solution)/shard_map/dot_general | solution.py:82
  85.5 61.6 %reduce-scatter.2.cloned.1.call-done = f32[192,1024]{1,0:T(8,128)} async-done(((f32[192,4096]{1,0:T(8,128)}), f32[192,1024]{1,0:T(8,128)}) %reduce-scatter.2.cloned.1.call-update) | async-done | bytes 786448 | tf_op jit(solution)/shard_map/reduce_scatter | solution.py:87
  147.1 2.0 %fusion.23 = bf16[1,192,1024]{2,1,0:T(8,128)(2,1)} fusion(f32[192,1024]{1,0:T(8,128)} %reduce-scatter.2.cloned.1.call-done, bf16[1,192,1024]{2,1,0:T(8,128)(2,1)S(1)} %copy-done.4), kind=kLoop, calls=%fused_computation.24 | loop fusion | flops 589824 | bytes 1572864 | tf_op jit(solution)/shard_map/broadcast_in_dim | solution.py:89
  (41 shorter events, 4.0 us)
Async XLA Ops:
  6.5 4.9 %copy-start = (s32[1,3,2]{1,2,0:T(2,128)S(1)}, s32[1,3,2]{1,2,0:T(2,128)}, u32[]{:S(2)}) copy-start(s32[1,3,2]{1,2,0:T(2,128)} %param.12) | copy-start | bytes 76
  6.5 3.7 %copy-start.6 = (u32[32]{0:T(128)S(1)}, u32[32]{0:T(128)}, u32[]{:S(2)}) copy-start(u32[32]{0:T(128)} %constant.96) | copy-start | bytes 388
  6.5 1.0 copy-start.3
  6.5 5.7 %copy-start.5 = (s32[1,3]{1,0:T(1,128)S(1)}, s32[1,3]{1,0:T(1,128)}, u32[]{:S(2)}) copy-start(s32[1,3]{1,0:T(1,128)} %param.13) | copy-start | bytes 40
  6.5 10.3 %copy-start.1 = (bf16[1,3,256,1024]{3,2,1,0:T(8,128)(2,1)S(1)}, bf16[1,3,256,1024]{3,2,1,0:T(8,128)(2,1)}, u32[]{:S(2)}) copy-start(bf16[1,3,256,1024]{3,2,1,0:T(8,128)(2,1)} %param.10) | copy-start | bytes 4718596
  6.5 72.0 %all-gather.3.cloned.1.call-start = ((), (), s32[]{:S(2)}) async-start(), calls=%async_computation.4 | async-start | bytes 10485760 | tf_op jit(solution)/shard_map/all_gather | solution.py:84
  8.7 14.0 %collective-permute-start = (bf16[3,64,1024]{2,0,1:T(4,128)(2,1)}, bf16[3,64,1024]{2,0,1:T(4,128)(2,1)}, u32[]{:S(2)}, u32[]{:S(2)}) collective-permute-start(bf16[3,64,1024]{2,0,1:T(4,128)(2,1)} %copy.31), channel_id=1, source_target_pairs={{0,16},{16,0},{1,17},{17,1},{2,18},{18,2},{3,19},{19,3},{4,20},{20... | collective-permute-start | bytes 1179656 | tf_op jit(solution)/shard_map/ppermute | solution.py:15
  25.1 16.6 %all-to-all-start = ((bf16[4,64,1024]{2,1,0:T(8,128)(2,1)}), bf16[4,64,1024]{2,1,0:T(8,128)(2,1)S(1)}, u32[]{:S(2)}, u32[]{:S(2)}) async-start(bf16[4,64,1024]{2,1,0:T(8,128)(2,1)} %copy.32), calls=%async_computation | async-start | bytes 1048576 | tf_op jit(solution)/shard_map/all_to_all | solution.py:73
  43.1 1.4 copy-start.2
  46.7 18.2 %all-to-all-start.1 = ((bf16[4,64,1024]{2,1,0:T(8,128)(2,1)}), bf16[4,64,1024]{2,1,0:T(8,128)(2,1)S(1)}, u32[]{:S(2)}, u32[]{:S(2)}) async-start(bf16[4,64,1024]{2,1,0:T(8,128)(2,1)} %copy.38), calls=%async_computation.1 | async-start | bytes 1048576 | tf_op jit(solution)/shard_map/all_to_all | solution.py:76
  52.1 95.0 %reduce-scatter.2.cloned.1.call-start = ((), (), s32[]{:S(2)}) async-start(), calls=%async_computation.3 | async-start | bytes 3932160 | tf_op jit(solution)/shard_map/reduce_scatter | solution.py:87
  65.7 11.2 %collective-permute-start.1 = (bf16[3,64,1024]{2,1,0:T(8,128)(2,1)S(1)}, bf16[3,64,1024]{2,1,0:T(8,128)(2,1)S(1)}, u32[]{:S(2)}, u32[]{:S(2)}) collective-permute-start(bf16[3,64,1024]{2,1,0:T(8,128)(2,1)S(1)} %broadcast_select_fusion), channel_id=1, source_target_pairs={{0,16},{16,0},{1,17},{17,1},{2,18},{18,2},{3,19},{19,3},{4,20},{20... | collective-permute-start | bytes 1179656 | tf_op jit(solution)/shard_map/ppermute | solution.py:15
  85.5 61.6 %copy-start.4 = (bf16[1,192,1024]{2,1,0:T(8,128)(2,1)S(1)}, bf16[1,192,1024]{2,1,0:T(8,128)(2,1)}, u32[]{:S(2)}) copy-start(bf16[1,192,1024]{2,1,0:T(8,128)(2,1)} %param.15) | copy-start | bytes 1179652
Sparse Core Ops, SparseCore 0:
  8.9 69.5 all-gather.2
  85.7 61.3 reduce-scatter.1
where the time goes:
time: 158 us; the launch traced here: 156 us
  waiting for transfers between devices  101 us (64%)
  between operations  14.2 us (9%)
  starting transfers between devices  12.5 us (8%)
  local copies, waits for them, and re-layouts  10.8 us (7%)
  matrix products  10 us (6%)
  blocking collectives  4.31 us (3%)
  other arithmetic  3.35 us (2%)
    reduce_scatter x1, waiting for transfers between devices, local(): lax.psum_scatter(partial_out, 'tp', scatter_dimension=1, tiled=True)  61.6 us
    all_to_all x1, waiting for transfers between devices, local(): lax.all_to_all(place(answer, anchors, count_dev), 'seq', split_axis=0, co...  12.9 us
    all_to_all x1, waiting for transfers between devices, local(): lax.all_to_all(outgoing, 'seq', split_axis=0, concat_axis=0, tiled=True)  12.8 us
    ppermute x2, waiting for transfers between devices, shifted(): lax.ppermute(value, axis, [(i, (i + by) % size) for i in range(size)])  11.1 us
    dot_general x1, matrix products, local(): jnp.dot(cca_rows, lax.all_gather(out_weight[0], 'seq', axis=1, tiled=True...  6.94 us
    unnamed x19, local copies, waits for them, and re-layouts  5.37 us
    all_to_all x1, starting transfers between devices, local(): lax.all_to_all(place(answer, anchors, count_dev), 'seq', split_axis=0, co...  5.33 us
    unnamed x1, blocking collectives  4.31 us
  transfers between devices with their start and end apart: 6, of which 6 were waited for; matrix products, arithmetic and copies ran while one was open for 9% of the time, Pallas kernels for 0%

commit v1 on v0

v1 whole, which is shorter than its diff:
```python
import math

import jax
import jax.numpy as jnp
from jax import lax
from jax.sharding import PartitionSpec as P

HD = 128
STRETCH = 64
NR = 128


def shifted(value, axis, by):
    size = lax.axis_size(axis)
    return lax.ppermute(value, axis, [(i, (i + by) % size) for i in range(size)])


def attend(query_rows, key_rows, value_rows, lengths):
    count, width, feats = query_rows.shape
    heads = feats // HD
    span = key_rows.shape[1]
    query_heads = query_rows.reshape(count, width, heads, HD)
    key_heads = key_rows.reshape(count, span, heads, HD)
    value_heads = value_rows.reshape(count, span, heads, HD)
    scores = jnp.einsum(
        "cqhd,clhd->chql", query_heads, key_heads, preferred_element_type=jnp.float32
    ) * (1.0 / math.sqrt(HD))
    position = jnp.arange(span, dtype=jnp.int32)
    limits = jnp.take(lengths, position // NR, axis=1)
    valid = ((position % NR)[None, :] < limits)[:, None, None, :]
    highest = jnp.max(jnp.where(valid, scores, -1e30), axis=-1, keepdims=True)
    expo = jnp.exp(jnp.where(valid, scores - highest, -1e30))
    weights = (expo / jnp.sum(expo, axis=-1, keepdims=True)).astype(jnp.bfloat16)
    mixed = jnp.einsum("chql,clhd->cqhd", weights, value_heads, preferred_element_type=jnp.float32)
    return mixed.astype(jnp.bfloat16).reshape(count, width, feats)


def local(queries, nb_keys, nb_values, nb_lengths, slot_stretch, out_weight, residual):
    count_dev = lax.axis_size("seq")
    seq_index = lax.axis_index("seq")
    per_dev = slot_stretch.shape[1]
    feats = queries.shape[2]
    rows = queries.shape[1]
    total = count_dev * per_dev
    mine = slot_stretch[0]
    lowered = shifted(queries[0].reshape(per_dev, STRETCH, feats), "segment", -1)
    spread = lax.all_gather(lowered, "seq", axis=0, tiled=True)
    picked = jnp.take(spread, mine, axis=0)
    answer = attend(picked, nb_keys[0], nb_values[0], nb_lengths[0])
    table_row = lax.all_gather(shifted(mine, "segment", 1), "seq", axis=0, tiled=True)
    answers = lax.all_gather(shifted(answer, "segment", 1), "seq", axis=0, tiled=True)
    stretch_ids = jnp.arange(total, dtype=jnp.int32)
    matched = table_row[None, :] == stretch_ids[:, None]
    slots = jnp.sum(jnp.where(matched, stretch_ids[None, :], 0), axis=1)
    cca = jnp.take(answers, slots, axis=0).reshape(total * STRETCH, feats)
    partial_out = jnp.dot(cca, out_weight[0], preferred_element_type=jnp.float32)
    blocks = partial_out.astype(jnp.bfloat16).reshape(count_dev, rows, out_weight.shape[2])
    columns = lax.all_to_all(blocks, "seq", split_axis=0, concat_axis=0, tiled=True)
    wide = columns.transpose(1, 0, 2).reshape(rows, -1)
    summed = lax.psum_scatter(wide.astype(jnp.float32), "tp", scatter_dimension=1, tiled=True)
    mixed = (residual[0].astype(jnp.float32) + summed).astype(jnp.bfloat16)
    return mixed[None]


def solution(mesh):
    in_specs = (
        P("segment", "seq", "tp"),
        P("segment", "seq", None, "tp"),
        P("segment", "seq", None, "tp"),
        P("segment", "seq", None),
        P("segment", "seq"),
        P("segment", "tp", "seq"),
        P("segment", "seq", "tp"),
    )
    out_specs = P("segment", "seq", "tp")
    return jax.shard_map(local, mesh=mesh, in_specs=in_specs, out_specs=out_specs, check_vma=False)
```

time: 158 us -> 180 us (1.14)
  blocking collectives: 4.31 us -> 27.7 us
  starting transfers between devices: 12.5 us -> 5.16 us
  matrix products: 10 us -> 2.95 us
  local copies, waits for them, and re-layouts: 10.8 us -> 17.7 us
  waiting for transfers between devices: 101 us -> 105 us
  other arithmetic: 3.35 us -> 5.19 us
    all_to_all x2 -> x0, waiting for transfers between devices: 25.7 us -> none  [the longest x1 12.9 us: local(): lax.all_to_all(place(answer, anchors, count_dev), 'seq', split_axis=0, co...]
    all_to_all x0 -> x1, blocking collectives: none -> 22.6 us  [local(): lax.all_to_all(blocks, 'seq', split_axis=0, concat_axis=0, tiled=True)]
    all_gather x1 -> x2, waiting for transfers between devices: 1.73 us -> 24.1 us  [the longest x1 13.4 us: local(): spread = lax.all_gather(lowered, 'seq', axis=0, tiled=True)]
    all_to_all x2 -> x0, starting transfers between devices: 9.08 us -> none  [the longest x1 5.33 us: local(): lax.all_to_all(place(answer, anchors, count_dev), 'seq', split_axis=0, co...]
    ppermute x2 -> x3, waiting for transfers between devices: 11.1 us -> 19.7 us  [shifted(): lax.ppermute(value, axis, [(i, (i + by) % size) for i in range(size)])]
    dot_general x3 -> x1, matrix products: 8.86 us -> 1.82 us  [local(): jnp.dot(cca, out_weight[0], preferred_element_type=jnp.float32)]
    gather x2, local copies, waits for them, and re-layouts: 1.14 us -> 5.24 us  [the longest x1 3.26 us: local(): cca = jnp.take(answers, slots, axis=0).reshape(total * STRETCH, feats)]
    unnamed x19 -> x24, local copies, waits for them, and re-layouts: 5.37 us -> 8.95 us
  transfers between devices with their start and end apart: 6 -> 6, of which waited for: 6 -> 6; matrix products, arithmetic and copies ran while one was open for 9% -> 4% of each run, Pallas kernels for 0% -> 0%
where the time goes in v1:
time: 180 us; the launch traced here: 178 us
  waiting for transfers between devices  105 us (58%)
  blocking collectives  27.7 us (15%)
  local copies, waits for them, and re-layouts  17.7 us (10%)
  between operations  13.9 us (8%)
  other arithmetic  5.19 us (3%)
  starting transfers between devices  5.16 us (3%)
  matrix products  2.95 us (2%)
    reduce_scatter x1, waiting for transfers between devices, local(): lax.psum_scatter(wide.astype(jnp.float32), 'tp', scatter_dimension=1, til...  61.5 us
    all_to_all x1, blocking collectives, local(): lax.all_to_all(blocks, 'seq', split_axis=0, concat_axis=0, tiled=True)  22.6 us
    ppermute x3, waiting for transfers between devices, shifted(): lax.ppermute(value, axis, [(i, (i + by) % size) for i in range(size)])  19.7 us
    all_gather x1, waiting for transfers between devices, local(): spread = lax.all_gather(lowered, 'seq', axis=0, tiled=True)  13.4 us
    all_gather x1, waiting for transfers between devices, local(): lax.all_gather(shifted(answer, 'segment', 1), 'seq', axis=0, tiled=True)  10.7 us
    unnamed x24, local copies, waits for them, and re-layouts  8.95 us
    unnamed x1, blocking collectives  5.12 us
    ppermute x3, starting transfers between devices, shifted(): lax.ppermute(value, axis, [(i, (i + by) % size) for i in range(size)])  5.08 us
  transfers between devices with their start and end apart: 6, of which 6 were waited for; matrix products, arithmetic and copies ran while one was open for 4% of the time, Pallas kernels for 0%

profile of v1, /device:TPU:2, one launch (start us, length us, event | category | flops | bytes accessed | tf_op | source)
XLA Modules:
  0.0 177.9 jit_solution(7871092805849377682)
XLA Ops:
  6.5 1.5 collective-permute-start.1
  8.1 9.5 %collective-permute-done.1 = bf16[3,64,1024]{2,1,0:T(8,128)(2,1)S(1)} collective-permute-done((bf16[3,64,1024]{2,1,0:T(8,128)(2,1)}, bf16[3,64,1024]{2,1,0:T(8,128)(2,1)S(1)}, u32[]{:S(2)}, u32[]{:S(2)}) %collective-permute-start.1) | collective-permute-done | bytes 393248 | tf_op jit(solution)/shard_map/ppermute | solution.py:15
  17.6 0.7 copy-done.5
  18.4 1.4 gather_fusion
  20.1 3.1 %copy.33 = bf16[96,8,8,128]{3,2,1,0:T(8,128)(2,1)} copy(bf16[96,8,8,128]{3,1,2,0:T(8,128)(2,1)} %bitcast.57) | data formatting | bytes 3145728
  23.3 1.6 copy.34
  24.9 13.4 %all-gather.3.cloned.1.call-done = bf16[12,64,1024]{2,1,0:T(8,128)(2,1)} async-done(((bf16[3,64,1024]{2,1,0:T(8,128)(2,1)}), bf16[12,64,1024]{2,1,0:T(8,128)(2,1)}) %all-gather.3.cloned.1.call-update) | async-done | bytes 1572880 | tf_op jit(solution)/shard_map/all_gather | solution.py:47
  38.3 2.0 %gather_fusion.1 = bf16[3,64,1024]{2,1,0:T(8,128)(2,1)S(1)} fusion(bf16[12,64,1024]{2,1,0:T(8,128)(2,1)} %all-gather.3.cloned.1.call-done, s32[1024]{0:T(1024)S(1)} %pad_clamp_fusion.1), kind=kCustom, calls=%fused_computation.1 | custom fusion | bytes 786444 | tf_op jit(solution)/shard_map/jit(_take)/gather | solution.py:48
  40.4 1.2 copy-done.1
  41.7 0.7 fusion.13
  42.3 0.8 fusion.33
  44.3 1.8 %collective-permute-start.2 = (bf16[3,64,1024]{2,1,0:T(8,128)(2,1)S(1)}, bf16[3,64,1024]{2,1,0:T(8,128)(2,1)S(1)}, u32[]{:S(2)}, u32[]{:S(2)}) collective-permute-start(bf16[3,64,1024]{2,1,0:T(8,128)(2,1)S(1)} %bitcast.65), channel_id=1, source_target_pairs={{0,16},{16,0},{1,17},{17,1},{2,18},{18,2},{3,19},{19,3},{4,20},{20... | collective-permute-start | bytes 1179656 | tf_op jit(solution)/shard_map/ppermute | solution.py:15
  46.1 9.5 %collective-permute-done.2 = bf16[3,64,1024]{2,1,0:T(8,128)(2,1)S(1)} collective-permute-done((bf16[3,64,1024]{2,1,0:T(8,128)(2,1)S(1)}, bf16[3,64,1024]{2,1,0:T(8,128)(2,1)S(1)}, u32[]{:S(2)}, u32[]{:S(2)}) %collective-permute-start.2) | collective-permute-done | bytes 393248 | tf_op jit(solution)/shard_map/ppermute | solution.py:15
  55.7 0.7 copy-done.4
  56.5 1.8 %collective-permute-start = (s32[3]{0:T(128)S(1)}, s32[3]{0:T(128)S(1)}, u32[]{:S(2)}, u32[]{:S(2)}) collective-permute-start(s32[3]{0:T(128)S(1)} %bitcast.68), channel_id=1, source_target_pairs={{0,16},{16,0},{1,17},{17,1},{2,18},{18,2},{3,19},{19,3},{4,20},{20... | collective-permute-start | bytes 44 | tf_op jit(solution)/shard_map/ppermute | solution.py:15
  60.3 5.1 %all-reduce = s32[12]{0:T(128)S(1)} all-reduce(s32[12]{0:T(128)S(1)} %dynamic-update-slice), channel_id=1, replica_groups=mesh['segment'=2,'seq'=4,'tp'=4] {'seq'}, use_global_device_ids=true, to_apply=%add | all-reduce | flops 12 | bytes 96
  65.5 10.7 %all-gather.5.cloned.1.call-done = bf16[12,64,1024]{2,1,0:T(8,128)(2,1)} async-done(((bf16[3,64,1024]{2,1,0:T(8,128)(2,1)}), bf16[12,64,1024]{2,1,0:T(8,128)(2,1)}) %all-gather.5.cloned.1.call-update) | async-done | bytes 1572880 | tf_op jit(solution)/shard_map/all_gather | solution.py:51
  76.2 3.3 %gather_fusion.2 = bf16[12,64,1024]{2,1,0:T(8,128)(2,1)} fusion(bf16[12,64,1024]{2,1,0:T(8,128)(2,1)} %all-gather.5.cloned.1.call-done, s32[1024]{0:T(1024)S(1)} %pad_clamp_fusion), kind=kCustom, calls=%fused_computation.2 | custom fusion | bytes 3145776 | tf_op jit(solution)/shard_map/jit(_take)/gather | solution.py:55
  79.5 1.6 broadcast_select_fusion
  81.1 1.8 %fusion.3 = bf16[768,1024]{1,0:T(8,128)(2,1)S(1)} fusion(bf16[768,1024]{1,0:T(8,128)(2,1)S(1)} %bitcast.63, bf16[1,1024,1024]{2,1,0:T(8,128)(2,1)S(1)} %copy-done), kind=kOutput, calls=%fused_computation.7 | convolution fusion | flops 1611399168 | bytes 5242880 | tf_op jit(solution)/shard_map/dot_general | solution.py:56
  83.0 22.6 %all_to_all.5 = bf16[4,192,1024]{2,1,0:T(8,128)(2,1)S(1)} all-to-all(bf16[4,192,1024]{2,1,0:T(8,128)(2,1)S(1)} %bitcast.60), channel_id=1, replica_groups=mesh['segment'=2,'seq'=4,'tp'=4] {'seq'}, dimensions={0} | all-to-all | bytes 3145728 | tf_op jit(solution)/shard_map/all_to_all | solution.py:58
  105.9 1.9 %copy.31 = f32[4,24,8,1024]{3,2,0,1:T(8,128)} copy(f32[4,24,8,1024]{3,2,1,0:T(8,128)S(1)} %convert_bitcast_fusion) | data formatting | bytes 6291456 | tf_op jit(solution)/shard_map/convert_element_type | solution.py:60
  107.8 61.5 %reduce-scatter.2.cloned.1.call-done = f32[192,1024]{1,0:T(8,128)} async-done(((f32[192,4096]{1,0:T(8,128)}), f32[192,1024]{1,0:T(8,128)}) %reduce-scatter.2.cloned.1.call-update) | async-done | bytes 786448 | tf_op jit(solution)/shard_map/reduce_scatter | solution.py:60
  169.4 2.0 %fusion.26 = bf16[1,192,1024]{2,1,0:T(8,128)(2,1)} fusion(f32[192,1024]{1,0:T(8,128)} %reduce-scatter.2.cloned.1.call-done, bf16[1,192,1024]{2,1,0:T(8,128)(2,1)S(1)} %copy-done.6), kind=kLoop, calls=%fused_computation.25 | loop fusion | flops 589824 | bytes 1572864 | tf_op jit(solution)/shard_map/broadcast_in_dim | solution.py:62
  (43 shorter events, 3.7 us)
Async XLA Ops:
  6.5 74.6 %copy-start = (bf16[1,1024,1024]{2,1,0:T(8,128)(2,1)S(1)}, bf16[1,1024,1024]{2,1,0:T(8,128)(2,1)}, u32[]{:S(2)}) copy-start(bf16[1,1024,1024]{2,1,0:T(8,128)(2,1)} %param.12) | copy-start | bytes 6291460
  6.5 31.7 %all-gather.3.cloned.1.call-start = ((), (), s32[]{:S(2)}) async-start(), calls=%async_computation.2 | async-start | bytes 1966080 | tf_op jit(solution)/shard_map/all_gather | solution.py:47
  6.5 11.1 %collective-permute-start.1 = (bf16[3,64,1024]{2,1,0:T(8,128)(2,1)}, bf16[3,64,1024]{2,1,0:T(8,128)(2,1)S(1)}, u32[]{:S(2)}, u32[]{:S(2)}) collective-permute-start(bf16[3,64,1024]{2,1,0:T(8,128)(2,1)} %bitcast.67), channel_id=1, source_target_pairs={{0,16},{16,0},{1,17},{17,1},{2,18},{18,2},{3,19},{19,3},{4,20},{20... | collective-permute-start | bytes 1179656 | tf_op jit(solution)/shard_map/ppermute | solution.py:15
  17.6 0.7 copy-start.5
  18.4 57.9 %all-gather.5.cloned.1.call-start = ((), (), s32[]{:S(2)}) async-start(), calls=%async_computation.3 | async-start | bytes 1966080 | tf_op jit(solution)/shard_map/all_gather | solution.py:51
  20.1 3.2 %copy-start.2 = (bf16[1,3,256,1024]{3,2,1,0:T(8,128)(2,1)S(1)}, bf16[1,3,256,1024]{3,2,1,0:T(8,128)(2,1)}, u32[]{:S(2)}) copy-start(bf16[1,3,256,1024]{3,2,1,0:T(8,128)(2,1)} %param.9) | copy-start | bytes 4718596
  23.3 1.6 copy-start.7
  40.3 1.4 copy-start.1
  42.3 1.4 copy-start.3
  43.7 14.5 %copy-start.8 = (u32[32]{0:T(128)S(1)}, u32[32]{0:T(128)}, u32[]{:S(2)}) copy-start(u32[32]{0:T(128)} %constant.92) | copy-start | bytes 388
  44.3 11.3 %collective-permute-start.2 = (bf16[3,64,1024]{2,1,0:T(8,128)(2,1)S(1)}, bf16[3,64,1024]{2,1,0:T(8,128)(2,1)S(1)}, u32[]{:S(2)}, u32[]{:S(2)}) collective-permute-start(bf16[3,64,1024]{2,1,0:T(8,128)(2,1)S(1)} %bitcast.65), channel_id=1, source_target_pairs={{0,16},{16,0},{1,17},{17,1},{2,18},{18,2},{3,19},{19,3},{4,20},{20... | collective-permute-start | bytes 1179656 | tf_op jit(solution)/shard_map/ppermute | solution.py:15
  55.6 0.7 copy-start.4
  56.4 112.9 %reduce-scatter.2.cloned.1.call-start = ((), (), s32[]{:S(2)}) async-start(), calls=%async_computation.4 | async-start | bytes 3932160 | tf_op jit(solution)/shard_map/reduce_scatter | solution.py:60
  56.5 3.6 %collective-permute-start = (s32[3]{0:T(128)S(1)}, s32[3]{0:T(128)S(1)}, u32[]{:S(2)}, u32[]{:S(2)}) collective-permute-start(s32[3]{0:T(128)S(1)} %bitcast.68), channel_id=1, source_target_pairs={{0,16},{16,0},{1,17},{17,1},{2,18},{18,2},{3,19},{19,3},{4,20},{20... | collective-permute-start | bytes 44 | tf_op jit(solution)/shard_map/ppermute | solution.py:15
  107.8 61.6 %copy-start.6 = (bf16[1,192,1024]{2,1,0:T(8,128)(2,1)S(1)}, bf16[1,192,1024]{2,1,0:T(8,128)(2,1)}, u32[]{:S(2)}) copy-start(bf16[1,192,1024]{2,1,0:T(8,128)(2,1)} %param.13) | copy-start | bytes 1179652
Sparse Core Ops, SparseCore 0:
  18.5 19.7 all-gather.2
  56.5 19.6 all-gather.4
  107.9 61.3 reduce-scatter.1

commit v2 on v1

v2 whole, which is shorter than its diff:
```python
import functools
import math

import jax
import jax.numpy as jnp
from jax import lax
from jax.experimental import pallas as pl
from jax.experimental.pallas import tpu as pltpu
from jax.sharding import PartitionSpec as P

HD = 128
STRETCH = 64
NR = 128
MESH = pl.DeviceIdType.MESH
F32 = jnp.float32
BF16 = jnp.bfloat16


def hops(count):
    steps, held = [], [0]
    bit = count // 2
    while bit:
        steps.append((bit, tuple(held)))
        held = held + [mask ^ bit for mask in held]
        bit //= 2
    return steps


def kernel(
    n_seg, n_seq, n_tp, per_dev,
    q_hbm, k_hbm, v_hbm, w_hbm, res_hbm, len_ref, slot_ref, table_ref,
    out_ref,
    kbuf, vbuf, wbuf, resbuf, qbuf, abuf, ans, psend, rbuf, upbuf, downbuf, tbuf, tsmem,
    load_sem, qy_send, qy_recv, qx_send, qx_recv, ay_send, ay_recv, ax_send, ax_recv,
    t_send, t_recv, p_send, p_recv, up_send, up_recv, down_send, down_recv,
):
    seg, seq, tp = lax.axis_index("segment"), lax.axis_index("seq"), lax.axis_index("tp")
    before = lax.rem(seg + n_seg - 1, n_seg)
    after = lax.rem(seg + 1, n_seg)
    span = k_hbm.shape[1]
    feats = q_hbm.shape[2]
    width = w_hbm.shape[1]
    ratio = n_seq // n_tp
    heads = feats // HD

    def xor(mask):
        out, bit = seq, 1
        while bit <= mask:
            if mask & bit:
                digit = lax.rem(lax.div(seq, bit), 2)
                out = out + bit - 2 * bit * digit
            bit *= 2
        return out

    partner = [xor(mask) for mask in range(n_seq)]

    loads = [
        pltpu.make_async_copy(src, dst, load_sem.at[i])
        for i, (src, dst) in enumerate(
            [(k_hbm, kbuf), (v_hbm, vbuf), (w_hbm, wbuf), (res_hbm, resbuf)]
        )
    ]

    barrier = pltpu.get_barrier_semaphore()

    def greet(device):
        pl.semaphore_signal(barrier, inc=1, device_id=device, device_id_type=MESH)

    sections = [after] if n_seg == 2 else [before, after]
    for mask in range(n_seq):
        for section in sections:
            greet((section, partner[mask], tp))
        if mask:
            greet((seg, partner[mask], tp))

    @pl.when(tp > 0)
    def _():
        greet((seg, seq, tp - 1))

    @pl.when(tp < n_tp - 1)
    def _():
        greet((seg, seq, tp + 1))

    for load in loads:
        load.start()
    line = jnp.int32(2) - (tp == 0).astype(jnp.int32) - (tp == n_tp - 1).astype(jnp.int32)
    pl.semaphore_wait(barrier, len(sections) * n_seq + n_seq - 1 + line)

    def remote(src, dst, send, recv, device):
        return pltpu.make_async_remote_copy(
            src_ref=src, dst_ref=dst, send_sem=send, recv_sem=recv,
            device_id=device, device_id_type=MESH,
        )

    pending = []

    qy = [
        remote(q_hbm.at[c], qbuf.at[seq * per_dev + c], qy_send.at[c], qy_recv.at[c], (before, seq, tp))
        for c in range(per_dev)
    ]
    for copy in qy:
        copy.start()
    pending += qy

    tables = [
        remote(table_ref, tbuf.at[seq], t_send.at[m], t_recv.at[m], (after, partner[m], tp))
        for m in range(n_seq)
    ]
    for copy in tables:
        copy.start()
    pending += tables

    steps = hops(n_seq)

    def spread(buf, send, recv, c):
        groups, at = [], 0
        for bit, held in steps:
            group = []
            for mask in held:
                place = buf.at[partner[mask] * per_dev + c]
                group.append(
                    remote(place, place, send.at[at, c], recv.at[at, c], (seg, partner[bit], tp))
                )
                at += 1
            groups.append(group)
        return groups

    def relay(first, groups):
        for c in range(per_dev):
            first[c].wait_recv()
            for group in groups[c]:
                group[0].start()
        for level in range(len(steps)):
            for c in range(per_dev):
                for at, copy in enumerate(groups[c][level]):
                    copy.wait_recv()
                    mask = steps[level][0] ^ steps[level][1][at]
                    for later in range(level + 1, len(steps)):
                        groups[c][later][steps[later][1].index(mask)].start()

    q_groups = [spread(qbuf, qx_send, qx_recv, c) for c in range(per_dev)]
    relay(qy, q_groups)
    pending += [copy for groups in q_groups for group in groups for copy in group]

    loads[0].wait()
    loads[1].wait()
    position = lax.broadcasted_iota(jnp.int32, (1, span), 1)
    ay = []
    for k in range(per_dev):
        limit = jnp.zeros((1, span), jnp.int32)
        for j in range(span // NR):
            inside = (position >= j * NR) & (position < (j + 1) * NR)
            limit = jnp.where(inside, j * NR + len_ref[k, j], limit)
        valid = position < limit
        stretch = slot_ref[0, k]
        for h in range(heads):
            cols = pl.ds(h * HD, HD)
            query = qbuf[stretch, :, cols]
            scores = lax.dot_general(
                query, kbuf[k, :, cols], (((1,), (1,)), ((), ())), preferred_element_type=F32
            ) * (1.0 / math.sqrt(HD))
            highest = jnp.max(jnp.where(valid, scores, -1e30), axis=1, keepdims=True)
            expo = jnp.exp(jnp.where(valid, scores - highest, -1e30))
            weights = (expo / jnp.sum(expo, axis=1, keepdims=True)).astype(BF16)
            ans[k, :, cols] = jnp.dot(
                weights, vbuf[k, :, cols], preferred_element_type=F32
            ).astype(BF16)
        copy = remote(
            ans.at[k], abuf.at[seq * per_dev + k], ay_send.at[k], ay_recv.at[k], (after, seq, tp)
        )
        copy.start()
        ay.append(copy)
    pending += ay

    a_groups = [spread(abuf, ax_send, ax_recv, c) for c in range(per_dev)]
    relay(ay, a_groups)
    pending += [copy for groups in a_groups for group in groups for copy in group]

    for copy in tables:
        copy.wait_recv()
    scalars = pltpu.make_async_copy(tbuf, tsmem, load_sem.at[4])
    scalars.start()
    scalars.wait()
    served = [tsmem[g // per_dev, 0, g % per_dev] for g in range(n_seq * per_dev)]

    def slot_of(stretch):
        slot = jnp.int32(0)
        for g, value in enumerate(served):
            slot = jnp.where(value == stretch, jnp.int32(g), slot)
        return slot

    loads[2].wait()
    order = list(range(n_seq - 1, -1, -1))
    if ratio == 1:
        mine = lambda c: rbuf.at[seq, c]
    else:
        lanes = pl.ds(pl.multiple_of(lax.rem(seq, ratio) * width, width), width)
        mine = lambda c: rbuf.at[lax.div(seq, ratio), c, :, lanes]
    exchange = {}
    for c in range(per_dev):
        rows = jnp.concatenate(
            [abuf[slot_of(partner[m] * per_dev + c)] for m in order], axis=0
        )
        product = jnp.dot(rows, wbuf[...], preferred_element_type=F32).astype(BF16)
        for at, m in enumerate(order):
            block = product[at * STRETCH:(at + 1) * STRETCH]
            if m == 0:
                mine(c)[...] = block
            else:
                psend[m - 1, c] = block
                copy = remote(
                    psend.at[m - 1, c], mine(c), p_send.at[m, c], p_recv.at[seq, c],
                    (seg, partner[m], tp),
                )
                copy.start()
                exchange[m, c] = copy

    last = n_tp - 1

    def arrived(target, c):
        for j in range(ratio):
            origin = target * ratio + j

            @pl.when(origin != seq)
            def _():
                remote(
                    psend.at[0, c], psend.at[0, c], p_send.at[0, c], p_recv.at[origin, c],
                    (seg, partner[1], tp),
                ).wait_recv()

    def along(buf, send, recv, c, d, device):
        return remote(buf.at[d, c], buf.at[d - 1, c], send.at[d, c], recv.at[d - 1, c], device)

    def here(buf, send, recv, c, d, device):
        return remote(buf.at[d, c], buf.at[d, c], send.at[d, c], recv.at[d, c], device)

    def push(buf, send, recv, c, d, target, first, device):
        arrived(target, c)

        @pl.when(first)
        def _():
            buf[d, c] = rbuf[target, c]

        if d < last:

            @pl.when(jnp.logical_not(first))
            def _():
                here(buf, send, recv, c, d, device).wait_recv()
                buf[d, c] = (buf[d, c].astype(F32) + rbuf[target, c].astype(F32)).astype(BF16)

        along(buf, send, recv, c, d, device).start()

    loads[3].wait()
    for c in range(per_dev):
        for d in range(last, 0, -1):
            @pl.when(tp + d <= last)
            def _():
                push(upbuf, up_send, up_recv, c, d, tp + d, tp == 0, (seg, seq, tp + 1))

            @pl.when(tp - d >= 0)
            def _():
                push(downbuf, down_send, down_recv, c, d, tp - d, tp == last, (seg, seq, tp - 1))
        arrived(tp, c)
        for buf, send, recv, end, near in (
            (upbuf, up_send, up_recv, 0, -1),
            (downbuf, down_send, down_recv, last, 1),
        ):
            @pl.when(tp == end)
            def _():
                buf[0, c] = jnp.zeros(buf.shape[2:], buf.dtype)

            @pl.when(tp != end)
            def _():
                here(buf, send, recv, c, 0, (seg, seq, tp + near)).wait_recv()
        own = pl.ds(c * STRETCH, STRETCH)
        total = upbuf[0, c].astype(F32) + downbuf[0, c].astype(F32) + rbuf[tp, c].astype(F32)
        out_ref[own, :] = (resbuf[own, :].astype(F32) + total).astype(out_ref.dtype)

    for copy in pending + list(exchange.values()):
        copy.wait_send()
    for c in range(per_dev):
        for d in range(last, 0, -1):
            @pl.when(tp + d <= last)
            def _():
                along(upbuf, up_send, up_recv, c, d, (seg, seq, tp + 1)).wait_send()

            @pl.when(tp - d >= 0)
            def _():
                along(downbuf, down_send, down_recv, c, d, (seg, seq, tp - 1)).wait_send()


def local(sizes, queries, nb_keys, nb_values, nb_lengths, slot_stretch, out_weight, residual):
    n_seg, n_seq, n_tp = sizes
    per_dev = slot_stretch.shape[1]
    rows, feats = queries.shape[1:]
    span = nb_keys.shape[2]
    width = out_weight.shape[2]
    keep = residual.shape[2]
    table = jnp.pad(slot_stretch, ((0, 7), (0, 128 - per_dev)))
    any_spec = pl.BlockSpec(memory_space=pl.ANY)
    smem_spec = pl.BlockSpec(memory_space=pltpu.SMEM)
    vmem_spec = pl.BlockSpec(memory_space=pltpu.VMEM)
    dma = pltpu.SemaphoreType.DMA
    block = (STRETCH, feats)
    mixed = pl.pallas_call(
        functools.partial(kernel, n_seg, n_seq, n_tp, per_dev),
        out_shape=jax.ShapeDtypeStruct((rows, keep), residual.dtype),
        in_specs=[any_spec] * 5 + [smem_spec] * 2 + [vmem_spec],
        out_specs=vmem_spec,
        scratch_shapes=[
            pltpu.VMEM((per_dev, span, feats), BF16),
            pltpu.VMEM((per_dev, span, feats), BF16),
            pltpu.VMEM((feats, width), BF16),
            pltpu.VMEM((rows, keep), BF16),
            pltpu.VMEM((n_seq * per_dev,) + block, BF16),
            pltpu.VMEM((n_seq * per_dev,) + block, BF16),
            pltpu.VMEM((per_dev,) + block, BF16),
            pltpu.VMEM((n_seq - 1, per_dev, STRETCH, width), BF16),
            pltpu.VMEM((n_tp, per_dev, STRETCH, keep), BF16),
            pltpu.VMEM((n_tp, per_dev, STRETCH, keep), BF16),
            pltpu.VMEM((n_tp, per_dev, STRETCH, keep), BF16),
            pltpu.VMEM((n_seq, 8, 128), jnp.int32),
            pltpu.SMEM((n_seq, 8, 128), jnp.int32),
            dma((5,)),
            dma((per_dev,)), dma((per_dev,)),
            dma((n_seq - 1, per_dev)), dma((n_seq - 1, per_dev)),
            dma((per_dev,)), dma((per_dev,)),
            dma((n_seq - 1, per_dev)), dma((n_seq - 1, per_dev)),
            dma((n_seq,)), dma((n_seq,)),
            dma((n_seq, per_dev)), dma((n_seq, per_dev)),
            dma((n_tp, per_dev)), dma((n_tp, per_dev)),
            dma((n_tp, per_dev)), dma((n_tp, per_dev)),
        ],
        compiler_params=pltpu.CompilerParams(
            collective_id=0, has_side_effects=True, vmem_limit_bytes=48 * 1024 * 1024
        ),
    )(
        queries.reshape(per_dev, STRETCH, feats), nb_keys[0], nb_values[0], out_weight[0],
        residual[0], nb_lengths[0], slot_stretch, table,
    )
    return mixed[None]


def solution(mesh):
    in_specs = (
        P("segment", "seq", "tp"),
        P("segment", "seq", None, "tp"),
        P("segment", "seq", None, "tp"),
        P("segment", "seq", None),
        P("segment", "seq"),
        P("segment", "tp", "seq"),
        P("segment", "seq", "tp"),
    )
    out_specs = P("segment", "seq", "tp")
    sizes = tuple(mesh.shape[name] for name in ("segment", "seq", "tp"))
    return jax.shard_map(
        functools.partial(local, sizes), mesh=mesh, in_specs=in_specs, out_specs=out_specs,
        check_vma=False,
    )
```

time: 180 us -> 95 us (0.53); the launches traced: 178 us -> 94.7 us
  waiting for transfers between devices: 105 us -> 0 us
  Pallas kernels: 0 us -> 87.1 us
  blocking collectives: 27.7 us -> 0 us
  between operations: 13.9 us -> 0.02 us
  local copies, waits for them, and re-layouts: 17.7 us -> 7.63 us
  other arithmetic: 5.19 us -> 0 us
  starting transfers between devices: 5.16 us -> 0 us
  matrix products: 2.95 us -> 0 us
    pallas_call x0 -> x1, Pallas kernels: none -> 87.1 us  [local(): pl.pallas_call(functools.partial(kernel, n_seg, n_seq, n_tp, per_dev), ou...]
    reduce_scatter x1 -> x0, waiting for transfers between devices: 61.5 us -> none  [local(): lax.psum_scatter(wide.astype(jnp.float32), 'tp', scatter_dimension=1, til...]
    all_gather x2 -> x0, waiting for transfers between devices: 24.1 us -> none  [the longest x1 13.4 us: local(): spread = lax.all_gather(lowered, 'seq', axis=0, tiled=True)]
    all_to_all x1 -> x0, blocking collectives: 22.6 us -> none  [local(): lax.all_to_all(blocks, 'seq', split_axis=0, concat_axis=0, tiled=True)]
    ppermute x3 -> x0, waiting for transfers between devices: 19.7 us -> none  [shifted(): lax.ppermute(value, axis, [(i, (i + by) % size) for i in range(size)])]
    gather x3 -> x0, local copies, waits for them, and re-layouts: 6.64 us -> none  [the longest x1 3.26 us: local(): cca = jnp.take(answers, slots, axis=0).reshape(total * STRETCH, feats)]
    unnamed x1 -> x0, blocking collectives: 5.12 us -> none
    ppermute x3 -> x0, starting transfers between devices: 5.08 us -> none  [shifted(): lax.ppermute(value, axis, [(i, (i + by) % size) for i in range(size)])]
  transfers between devices with their start and end apart: 6 -> 0, of which waited for: 6 -> 0; matrix products, arithmetic and copies ran while one was open for 4% -> 0% of each run, Pallas kernels for 0% -> 0%
where the time goes in v2:
time: 95 us; the launch traced here: 94.7 us
  Pallas kernels  87.1 us (92%)
  local copies, waits for them, and re-layouts  7.63 us (8%)
    pallas_call x1, Pallas kernels, local(): pl.pallas_call(functools.partial(kernel, n_seg, n_seq, n_tp, per_dev), ou...  87.1 us
    unnamed x11, local copies, waits for them, and re-layouts  6.21 us

profile of v2, /device:TPU:2, one launch (start us, length us, event | category | flops | bytes accessed | tf_op | source)
XLA Modules:
  0.0 94.7 jit_solution(6854703259446599172)
XLA Ops:
  0.0 0.8 copy.8.len_ref
  0.8 0.7 pad.4.table_ref
  1.4 0.0 copy-start
  1.4 1.4 %copy-done = bf16[1,3,256,1024]{3,2,1,0:T(8,128)(2,1)S(1)} copy-done((bf16[1,3,256,1024]{3,2,1,0:T(8,128)(2,1)S(1)}, bf16[1,3,256,1024]{3,2,1,0:T(8,128)(2,1)}, u32[]{:S(2)}) %copy-start) | copy-done | bytes 1572888
  2.8 0.0 copy-start.1
  2.8 1.4 %copy-done.1 = bf16[1,3,256,1024]{3,2,1,0:T(8,128)(2,1)S(1)} copy-done((bf16[1,3,256,1024]{3,2,1,0:T(8,128)(2,1)S(1)}, bf16[1,3,256,1024]{3,2,1,0:T(8,128)(2,1)}, u32[]{:S(2)}) %copy-start.1) | copy-done | bytes 1572888
  4.2 0.0 copy-start.2
  4.2 1.0 %copy-done.2 = bf16[1,192,1024]{2,1,0:T(8,128)(2,1)S(1)} copy-done((bf16[1,192,1024]{2,1,0:T(8,128)(2,1)S(1)}, bf16[1,192,1024]{2,1,0:T(8,128)(2,1)}, u32[]{:S(2)}) %copy-start.2) | copy-done | bytes 393240
  5.2 0.0 copy-start.3
  5.2 1.0 %copy-done.3 = bf16[1,192,1024]{2,1,0:T(8,128)(2,1)S(1)} copy-done((bf16[1,192,1024]{2,1,0:T(8,128)(2,1)S(1)}, bf16[1,192,1024]{2,1,0:T(8,128)(2,1)}, u32[]{:S(2)}) %copy-start.3) | copy-done | bytes 393240
  6.2 0.0 copy-start.4
  6.2 0.7 copy-done.4
  6.9 87.1 %shard_map.73 = bf16[192,1024]{1,0:T(8,128)(2,1)S(1)} custom-call(bf16[3,64,1024]{2,1,0:T(8,128)(2,1)S(1)} %bitcast.10, bf16[3,256,1024]{2,1,0:T(8,128)(2,1)S(1)} %bitcast.7, bf16[3,256,1024]{2,1,0:T(8,128)(2,1)S(1)} %bitcast.8, bf16[1024,1024]{1,0:T(8,128)(2,1)} %bitcast.12, bf16[192,1024]{1,0:T(8,128)(2,1)S(1)} %bitcast.11, s32[3,2]{1,0:T(4,128)S(1)} %copy.8.len_ref, ...), custom_call_target="tpu_custom_call" | custom-call | tf_op jit(solution)/shard_map/pallas_call | solution.py:305
  94.0 0.7 copy.10
Async XLA Ops:
  1.4 1.4 %copy-start = (bf16[1,3,256,1024]{3,2,1,0:T(8,128)(2,1)S(1)}, bf16[1,3,256,1024]{3,2,1,0:T(8,128)(2,1)}, u32[]{:S(2)}) copy-start(bf16[1,3,256,1024]{3,2,1,0:T(8,128)(2,1)} %param.8) | copy-start | bytes 4718596
  2.8 1.4 %copy-start.1 = (bf16[1,3,256,1024]{3,2,1,0:T(8,128)(2,1)S(1)}, bf16[1,3,256,1024]{3,2,1,0:T(8,128)(2,1)}, u32[]{:S(2)}) copy-start(bf16[1,3,256,1024]{3,2,1,0:T(8,128)(2,1)} %param.9) | copy-start | bytes 4718596
  4.2 1.0 %copy-start.2 = (bf16[1,192,1024]{2,1,0:T(8,128)(2,1)S(1)}, bf16[1,192,1024]{2,1,0:T(8,128)(2,1)}, u32[]{:S(2)}) copy-start(bf16[1,192,1024]{2,1,0:T(8,128)(2,1)} %param.7) | copy-start | bytes 1179652
  5.2 1.0 %copy-start.3 = (bf16[1,192,1024]{2,1,0:T(8,128)(2,1)S(1)}, bf16[1,192,1024]{2,1,0:T(8,128)(2,1)}, u32[]{:S(2)}) copy-start(bf16[1,192,1024]{2,1,0:T(8,128)(2,1)} %param.13) | copy-start | bytes 1179652
  6.2 0.7 copy-start.4

commit v3 on v2

v3 whole, which is shorter than its diff:
```python
import functools
import math

import jax
import jax.numpy as jnp
from jax import lax
from jax.experimental import pallas as pl
from jax.experimental.pallas import tpu as pltpu
from jax.sharding import PartitionSpec as P

HD = 128
STRETCH = 64
NR = 128
GROUPS = 4
MESH = pl.DeviceIdType.MESH
F32 = jnp.float32
BF16 = jnp.bfloat16


def hops(count):
    steps, held = [], [0]
    bit = count // 2
    while bit:
        steps.append((bit, tuple(held)))
        held = held + [mask ^ bit for mask in held]
        bit //= 2
    return steps


def kernel(
    n_seg, n_seq, n_tp, per_dev,
    q_hbm, k_hbm, v_hbm, w_hbm, res_hbm, table_ref,
    out_ref,
    kbuf, vbuf, wbuf, resbuf, qbufs, abufs, answers, acc, psend, rbuf, upbuf, downbuf, tbuf, tsmem, own_smem,
    load_sem, qy_send, qy_recv, qx_send, qx_recv, ay_send, ay_recv, ax_send, ax_recv,
    t_send, t_recv, p_send, p_recv, up_send, up_recv, down_send, down_recv,
):
    seg, seq, tp = lax.axis_index("segment"), lax.axis_index("seq"), lax.axis_index("tp")
    before = lax.rem(seg + n_seg - 1, n_seg)
    after = lax.rem(seg + 1, n_seg)
    span = k_hbm.shape[1]
    feats = q_hbm.shape[2]
    width = w_hbm.shape[1]
    ratio = n_seq // n_tp
    groups = len(qbufs)
    part = feats // groups

    def xor(mask):
        out, bit = seq, 1
        while bit <= mask:
            if mask & bit:
                digit = lax.rem(lax.div(seq, bit), 2)
                out = out + bit - 2 * bit * digit
            bit *= 2
        return out

    partner = [xor(mask) for mask in range(n_seq)]

    loads = [
        pltpu.make_async_copy(src, dst, load_sem.at[i])
        for i, (src, dst) in enumerate(
            [(k_hbm, kbuf), (v_hbm, vbuf), (w_hbm, wbuf), (res_hbm, resbuf), (table_ref, own_smem)]
        )
    ]

    barrier = pltpu.get_barrier_semaphore()

    def greet(device):
        pl.semaphore_signal(barrier, inc=1, device_id=device, device_id_type=MESH)

    sections = [after] if n_seg == 2 else [before, after]
    for mask in range(n_seq):
        for section in sections:
            greet((section, partner[mask], tp))
        if mask:
            greet((seg, partner[mask], tp))

    @pl.when(tp > 0)
    def _():
        greet((seg, seq, tp - 1))

    @pl.when(tp < n_tp - 1)
    def _():
        greet((seg, seq, tp + 1))

    for load in loads:
        load.start()
    line = jnp.int32(2) - (tp == 0).astype(jnp.int32) - (tp == n_tp - 1).astype(jnp.int32)
    pl.semaphore_wait(barrier, len(sections) * n_seq + n_seq - 1 + line)

    def remote(src, dst, send, recv, device):
        return pltpu.make_async_remote_copy(
            src_ref=src, dst_ref=dst, send_sem=send, recv_sem=recv,
            device_id=device, device_id_type=MESH,
        )

    pending = []

    own_rows = pl.ds(seq * per_dev, per_dev)
    qy = [
        remote(
            q_hbm.at[:, :, pl.ds(g * part, part)], qbufs[g].at[own_rows],
            qy_send.at[g], qy_recv.at[g], (before, seq, tp),
        )
        for g in range(groups)
    ]
    for copy in qy:
        copy.start()
    pending += qy

    tables = [
        remote(table_ref, tbuf.at[seq], t_send.at[m], t_recv.at[m], (after, partner[m], tp))
        for m in range(n_seq)
    ]
    for copy in tables:
        copy.start()
    pending += tables

    steps = hops(n_seq)

    def spread(buf, send, recv, g):
        levels, at = [], 0
        for bit, held in steps:
            level = []
            for mask in held:
                place = buf.at[pl.ds(partner[mask] * per_dev, per_dev)]
                level.append(
                    remote(place, place, send.at[at, g], recv.at[at, g], (seg, partner[bit], tp))
                )
                at += 1
            levels.append(level)
        return levels

    def enter(first, levels):
        first.wait_recv()
        for level in levels:
            level[0].start()

    def relay(levels, depth):
        bit, held = steps[depth]
        for mask, copy in zip(held, levels[depth]):
            copy.wait_recv()
            for later in range(depth + 1, len(steps)):
                levels[later][steps[later][1].index(mask ^ bit)].start()

    q_levels = [spread(qbufs[g], qx_send, qx_recv, g) for g in range(groups)]
    a_levels = [spread(abufs[g], ax_send, ax_recv, g) for g in range(groups)]
    ay = [
        remote(answers[g], abufs[g].at[own_rows], ay_send.at[g], ay_recv.at[g], (after, seq, tp))
        for g in range(groups)
    ]
    pending += [copy for levels in q_levels + a_levels for level in levels for copy in level]
    pending += ay

    position = lax.broadcasted_iota(jnp.int32, (1, span), 1)

    def attend(g):
        if g == 0:
            loads[4].wait()
            loads[0].wait()
            loads[1].wait()
        for k in range(per_dev):
            limit = jnp.zeros((1, span), jnp.int32)
            for j in range(span // NR):
                inside = (position >= j * NR) & (position < (j + 1) * NR)
                limit = jnp.where(inside, j * NR + own_smem[1 + k, j], limit)
            valid = position < limit
            stretch = own_smem[0, k]
            for h in range(part // HD):
                cols = pl.ds(h * HD, HD)
                wide = pl.ds(g * part + h * HD, HD)
                query = qbufs[g][stretch, :, cols]
                scores = lax.dot_general(
                    query, kbuf[k, :, wide], (((1,), (1,)), ((), ())), preferred_element_type=F32
                ) * (1.0 / math.sqrt(HD))
                highest = jnp.max(jnp.where(valid, scores, -1e30), axis=1, keepdims=True)
                expo = jnp.exp(jnp.where(valid, scores - highest, -1e30))
                weights = (expo / jnp.sum(expo, axis=1, keepdims=True)).astype(BF16)
                answers[g][k, :, cols] = jnp.dot(
                    weights, vbuf[k, :, wide], preferred_element_type=F32
                ).astype(BF16)
        ay[g].start()

    order = list(range(n_seq - 1, -1, -1))
    if ratio == 1:
        mine = lambda c: rbuf.at[seq, c]
    else:
        lanes = pl.ds(pl.multiple_of(lax.rem(seq, ratio) * width, width), width)
        mine = lambda c: rbuf.at[lax.div(seq, ratio), c, :, lanes]
    exchange = {}
    slots = {}

    def find_slots():
        for copy in tables:
            copy.wait_recv()
        scalars = pltpu.make_async_copy(tbuf, tsmem, load_sem.at[5])
        scalars.start()
        scalars.wait()
        served = [tsmem[g // per_dev, 0, g % per_dev] for g in range(n_seq * per_dev)]
        for m in order:
            for c in range(per_dev):
                slot = jnp.int32(0)
                for g, value in enumerate(served):
                    slot = jnp.where(value == partner[m] * per_dev + c, jnp.int32(g), slot)
                slots[m, c] = slot

    def project(g):
        if g == 0:
            find_slots()
            loads[2].wait()
        for c in range(per_dev):
            rows = jnp.concatenate([abufs[g][slots[m, c]] for m in order], axis=0)
            product = jnp.dot(
                rows, wbuf[pl.ds(g * part, part), :], preferred_element_type=F32
            )
            if g:
                product = acc[c] + product
            if g < groups - 1:
                acc[c] = product
                continue
            product = product.astype(BF16)
            for at, m in enumerate(order):
                block = product[at * STRETCH:(at + 1) * STRETCH]
                if m == 0:
                    mine(c)[...] = block
                else:
                    psend[m - 1, c] = block
                    copy = remote(
                        psend.at[m - 1, c], mine(c), p_send.at[m, c], p_recv.at[seq, c],
                        (seg, partner[m], tp),
                    )
                    copy.start()
                    exchange[m, c] = copy

    depth = len(steps)
    stages = [lambda g: enter(qy[g], q_levels[g])]
    stages += [lambda g, d=d: relay(q_levels[g], d) for d in range(depth)]
    stages[-1] = lambda g: (relay(q_levels[g], depth - 1), attend(g))
    stages += [lambda g: enter(ay[g], a_levels[g])]
    stages += [lambda g, d=d: relay(a_levels[g], d) for d in range(depth)]
    stages[-1] = lambda g: (relay(a_levels[g], depth - 1), project(g))
    delay = [at + (at > depth) for at in range(len(stages))]
    for turn in range(groups + delay[-1]):
        for stage, late in zip(stages, delay):
            if 0 <= turn - late < groups:
                stage(turn - late)

    last = n_tp - 1

    def arrived(target, c):
        for j in range(ratio):
            origin = target * ratio + j

            @pl.when(origin != seq)
            def _():
                remote(
                    psend.at[0, c], psend.at[0, c], p_send.at[0, c], p_recv.at[origin, c],
                    (seg, partner[1], tp),
                ).wait_recv()

    def along(buf, send, recv, c, target, device):
        place = buf.at[target, c]
        return remote(place, place, send.at[target, c], recv.at[target, c], device)

    def push(buf, send, recv, c, target, first, device):
        @pl.when(first)
        def _():
            buf[target, c] = rbuf[target, c]

        @pl.when(jnp.logical_not(first))
        def _():
            along(buf, send, recv, c, target, device).wait_recv()
            buf[target, c] = (buf[target, c].astype(F32) + rbuf[target, c].astype(F32)).astype(BF16)

        along(buf, send, recv, c, target, device).start()

    def finish(c):
        for buf, send, recv, end, near in (
            (upbuf, up_send, up_recv, 0, -1),
            (downbuf, down_send, down_recv, last, 1),
        ):
            @pl.when(tp == end)
            def _():
                buf[tp, c] = jnp.zeros(buf.shape[2:], buf.dtype)

            @pl.when(tp != end)
            def _():
                along(buf, send, recv, c, tp, (seg, seq, tp + near)).wait_recv()
        own = pl.ds(c * STRETCH, STRETCH)
        total = upbuf[tp, c].astype(F32) + downbuf[tp, c].astype(F32) + rbuf[tp, c].astype(F32)
        out_ref[own, :] = (resbuf[own, :].astype(F32) + total).astype(out_ref.dtype)

    home = lax.div(seq, ratio)
    near = n_tp // 2
    visits = [(m, c) for m in range(near) for c in range(per_dev)]
    visits += [(m, c) for c in range(per_dev) for m in range(n_tp - 1, near - 1, -1)]
    targets = {}
    for m in range(n_tp):
        target, bit = home, 1
        while bit <= m:
            if m & bit:
                target = target + bit - 2 * bit * lax.rem(lax.div(home, bit), 2)
            bit *= 2
        targets[m] = target
    loads[3].wait()
    for m, c in visits:
        target = targets[m]
        arrived(target, c)

        @pl.when(target > tp)
        def _():
            push(upbuf, up_send, up_recv, c, target, tp == 0, (seg, seq, tp + 1))

        @pl.when(target < tp)
        def _():
            push(downbuf, down_send, down_recv, c, target, tp == last, (seg, seq, tp - 1))

    for c in range(per_dev):
        finish(c)

    for copy in pending + list(exchange.values()):
        copy.wait_send()
    for m, c in visits:
        target = targets[m]

        @pl.when(target > tp)
        def _():
            along(upbuf, up_send, up_recv, c, target, (seg, seq, tp + 1)).wait_send()

        @pl.when(target < tp)
        def _():
            along(downbuf, down_send, down_recv, c, target, (seg, seq, tp - 1)).wait_send()


def local(sizes, queries, nb_keys, nb_values, nb_lengths, slot_stretch, out_weight, residual):
    n_seg, n_seq, n_tp = sizes
    per_dev = slot_stretch.shape[1]
    rows, feats = queries.shape[1:]
    span = nb_keys.shape[2]
    width = out_weight.shape[2]
    keep = residual.shape[2]
    lengths = nb_lengths[0]
    table = jnp.pad(slot_stretch, ((0, 7), (0, 128 - per_dev)))
    table += jnp.pad(lengths, ((1, 7 - per_dev), (0, 128 - lengths.shape[1])))
    any_spec = pl.BlockSpec(memory_space=pl.ANY)
    vmem_spec = pl.BlockSpec(memory_space=pltpu.VMEM)
    dma = pltpu.SemaphoreType.DMA
    block = (STRETCH, feats // GROUPS)
    mixed = pl.pallas_call(
        functools.partial(kernel, n_seg, n_seq, n_tp, per_dev),
        out_shape=jax.ShapeDtypeStruct((rows, keep), residual.dtype),
        in_specs=[any_spec] * 5 + [vmem_spec],
        out_specs=vmem_spec,
        scratch_shapes=[
            pltpu.VMEM((per_dev, span, feats), BF16),
            pltpu.VMEM((per_dev, span, feats), BF16),
            pltpu.VMEM((feats, width), BF16),
            pltpu.VMEM((rows, keep), BF16),
            [pltpu.VMEM((n_seq * per_dev,) + block, BF16)] * GROUPS,
            [pltpu.VMEM((n_seq * per_dev,) + block, BF16)] * GROUPS,
            [pltpu.VMEM((per_dev,) + block, BF16)] * GROUPS,
            pltpu.VMEM((per_dev, n_seq * STRETCH, width), F32),
            pltpu.VMEM((n_seq - 1, per_dev, STRETCH, width), BF16),
            pltpu.VMEM((n_tp, per_dev, STRETCH, keep), BF16),
            pltpu.VMEM((n_tp, per_dev, STRETCH, keep), BF16),
            pltpu.VMEM((n_tp, per_dev, STRETCH, keep), BF16),
            pltpu.VMEM((n_seq, 8, 128), jnp.int32),
            pltpu.SMEM((n_seq, 8, 128), jnp.int32),
            pltpu.SMEM((8, 128), jnp.int32),
            dma((6,)),
            dma((GROUPS,)), dma((GROUPS,)),
            dma((n_seq - 1, GROUPS)), dma((n_seq - 1, GROUPS)),
            dma((GROUPS,)), dma((GROUPS,)),
            dma((n_seq - 1, GROUPS)), dma((n_seq - 1, GROUPS)),
            dma((n_seq,)), dma((n_seq,)),
            dma((n_seq, per_dev)), dma((n_seq, per_dev)),
            dma((n_tp, per_dev)), dma((n_tp, per_dev)),
            dma((n_tp, per_dev)), dma((n_tp, per_dev)),
        ],
        compiler_params=pltpu.CompilerParams(
            collective_id=0, has_side_effects=True, vmem_limit_bytes=60 * 1024 * 1024
        ),
    )(
        queries.reshape(per_dev, STRETCH, feats), nb_keys[0], nb_values[0], out_weight[0],
        residual[0], table,
    )
    return mixed[None]


def solution(mesh):
    in_specs = (
        P("segment", "seq", "tp"),
        P("segment", "seq", None, "tp"),
        P("segment", "seq", None, "tp"),
        P("segment", "seq", None),
        P("segment", "seq"),
        P("segment", "tp", "seq"),
        P("segment", "seq", "tp"),
    )
    out_specs = P("segment", "seq", "tp")
    sizes = tuple(mesh.shape[name] for name in ("segment", "seq", "tp"))
    return jax.shard_map(
        functools.partial(local, sizes), mesh=mesh, in_specs=in_specs, out_specs=out_specs,
        check_vma=False,
    )
```

time: 95 us -> 83.4 us (0.88)
  Pallas kernels: 87.1 us -> 79.4 us
  local copies, waits for them, and re-layouts: 7.63 us -> 2.53 us
  other arithmetic: 0 us -> 1.25 us
    pallas_call x1, Pallas kernels: 87.1 us -> 79.4 us  [local(): pl.pallas_call(functools.partial(kernel, n_seg, n_seq, n_tp, per_dev), ou...]
    unnamed x11 -> x1, local copies, waits for them, and re-layouts: 6.21 us -> 1.77 us
    add x0 -> x1, other arithmetic: none -> 1.25 us  [local(): table += jnp.pad(lengths, ((1, 7 - per_dev), (0, 128 - lengths.shape[1])))]
where the time goes in v3:
time: 83.4 us; the launch traced here: 83.2 us
  Pallas kernels  79.4 us (95%)
  local copies, waits for them, and re-layouts  2.53 us (3%)
  other arithmetic  1.25 us (1%)
    pallas_call x1, Pallas kernels, local(): pl.pallas_call(functools.partial(kernel, n_seg, n_seq, n_tp, per_dev), ou...  79.4 us
    unnamed x1, local copies, waits for them, and re-layouts  1.77 us

profile of v3, /device:TPU:2, one launch (start us, length us, event | category | flops | bytes accessed | tf_op | source)
XLA Modules:
  0.0 83.2 jit_solution(7327686812053280788)
XLA Ops:
  0.0 0.8 copy.8
  0.8 1.3 %pad_add_fusion.table_ref = s32[8,128]{1,0:T(8,128)} fusion(s32[3,2]{1,0:T(4,128)S(1)} %copy.8, s32[1,3]{1,0:T(1,128)} %param.11), kind=kLoop, calls=%fused_computation | loop fusion | flops 1024 | bytes 4132 | tf_op jit(solution)/shard_map/add | solution.py:344
  2.0 79.4 %shard_map.73 = bf16[192,1024]{1,0:T(8,128)(2,1)} custom-call(bf16[3,64,1024]{2,1,0:T(8,128)(2,1)} %bitcast.11, bf16[3,256,1024]{2,1,0:T(8,128)(2,1)} %bitcast.8, bf16[3,256,1024]{2,1,0:T(8,128)(2,1)} %bitcast.9, bf16[1024,1024]{1,0:T(8,128)(2,1)} %bitcast.7, bf16[192,1024]{1,0:T(8,128)(2,1)} %bitcast.12, s32[8,128]{1,0:T(8,128)} %pad_add_fusion.table_ref), custom_call_target="tpu_custom_call" | custom-call | tf_op jit(solution)/shard_map/pallas_call | solution.py:349
  81.4 1.8 %copy.10 = bf16[1,192,1024]{2,1,0:T(8,128)(2,1)} copy(bf16[1,192,1024]{2,1,0:T(8,128)(2,1)} %bitcast.10) | data formatting | bytes 786432

commit v4 on v3

--- a/solution.py
+++ b/solution.py
@@ -29,9 +29,9 @@
 
 def kernel(
     n_seg, n_seq, n_tp, per_dev,
-    q_hbm, k_hbm, v_hbm, w_hbm, res_hbm, table_ref,
+    q_hbm, k_hbm, v_hbm, w_hbm, res_hbm, len_ref, slot_ref, row_ref,
     out_ref,
-    kbuf, vbuf, wbuf, resbuf, qbufs, abufs, answers, acc, psend, rbuf, upbuf, downbuf, tbuf, tsmem, own_smem,
+    kbuf, vbuf, wbuf, resbuf, qbufs, abufs, answers, acc, psend, rbuf, upbuf, downbuf, table, tbuf, tsmem,
     load_sem, qy_send, qy_recv, qx_send, qx_recv, ay_send, ay_recv, ax_send, ax_recv,
     t_send, t_recv, p_send, p_recv, up_send, up_recv, down_send, down_recv,
 ):
@@ -59,7 +59,7 @@
     loads = [
         pltpu.make_async_copy(src, dst, load_sem.at[i])
         for i, (src, dst) in enumerate(
-            [(k_hbm, kbuf), (v_hbm, vbuf), (w_hbm, wbuf), (res_hbm, resbuf), (table_ref, own_smem)]
+            [(k_hbm, kbuf), (v_hbm, vbuf), (w_hbm, wbuf), (res_hbm, resbuf)]
         )
     ]
 
@@ -85,6 +85,8 @@
 
     for load in loads:
         load.start()
+    table[...] = jnp.zeros(table.shape, table.dtype)
+    table[0:1, 0:per_dev] = row_ref[...]
     line = jnp.int32(2) - (tp == 0).astype(jnp.int32) - (tp == n_tp - 1).astype(jnp.int32)
     pl.semaphore_wait(barrier, len(sections) * n_seq + n_seq - 1 + line)
 
@@ -109,7 +111,7 @@
     pending += qy
 
     tables = [
-        remote(table_ref, tbuf.at[seq], t_send.at[m], t_recv.at[m], (after, partner[m], tp))
+        remote(table, tbuf.at[seq], t_send.at[m], t_recv.at[m], (after, partner[m], tp))
         for m in range(n_seq)
     ]
     for copy in tables:
@@ -156,16 +158,15 @@
 
     def attend(g):
         if g == 0:
-            loads[4].wait()
             loads[0].wait()
             loads[1].wait()
         for k in range(per_dev):
             limit = jnp.zeros((1, span), jnp.int32)
             for j in range(span // NR):
                 inside = (position >= j * NR) & (position < (j + 1) * NR)
-                limit = jnp.where(inside, j * NR + own_smem[1 + k, j], limit)
+                limit = jnp.where(inside, j * NR + len_ref[j, k], limit)
             valid = position < limit
-            stretch = own_smem[0, k]
+            stretch = slot_ref[0, k]
             for h in range(part // HD):
                 cols = pl.ds(h * HD, HD)
                 wide = pl.ds(g * part + h * HD, HD)
@@ -173,9 +174,9 @@
                 scores = lax.dot_general(
                     query, kbuf[k, :, wide], (((1,), (1,)), ((), ())), preferred_element_type=F32
                 ) * (1.0 / math.sqrt(HD))
-                highest = jnp.max(jnp.where(valid, scores, -1e30), axis=1, keepdims=True)
-                expo = jnp.exp(jnp.where(valid, scores - highest, -1e30))
-                weights = (expo / jnp.sum(expo, axis=1, keepdims=True)).astype(BF16)
+                scores = jnp.where(valid, scores, -1e30)
+                expo = jnp.exp(scores - jnp.max(scores, axis=1, keepdims=True))
+                weights = (expo * (1.0 / jnp.sum(expo, axis=1, keepdims=True))).astype(BF16)
                 answers[g][k, :, cols] = jnp.dot(
                     weights, vbuf[k, :, wide], preferred_element_type=F32
                 ).astype(BF16)
@@ -193,7 +194,7 @@
     def find_slots():
         for copy in tables:
             copy.wait_recv()
-        scalars = pltpu.make_async_copy(tbuf, tsmem, load_sem.at[5])
+        scalars = pltpu.make_async_copy(tbuf, tsmem, load_sem.at[4])
         scalars.start()
         scalars.wait()
         served = [tsmem[g // per_dev, 0, g % per_dev] for g in range(n_seq * per_dev)]
@@ -292,16 +293,11 @@
 
     home = lax.div(seq, ratio)
     near = n_tp // 2
-    visits = [(m, c) for m in range(near) for c in range(per_dev)]
-    visits += [(m, c) for c in range(per_dev) for m in range(n_tp - 1, near - 1, -1)]
-    targets = {}
-    for m in range(n_tp):
-        target, bit = home, 1
-        while bit <= m:
-            if m & bit:
-                target = target + bit - 2 * bit * lax.rem(lax.div(home, bit), 2)
-            bit *= 2
-        targets[m] = target
+    low = home < near
+    targets = [jnp.where(low, p, last - p) for p in range(near)]
+    targets += [jnp.where(low, last - p, p) for p in range(near)]
+    visits = [(m, c) for c in range(per_dev) for m in range(near)]
+    visits += [(m, c) for c in range(per_dev) for m in range(near, n_tp)]
     loads[3].wait()
     for m, c in visits:
         target = targets[m]
@@ -339,17 +335,15 @@
     span = nb_keys.shape[2]
     width = out_weight.shape[2]
     keep = residual.shape[2]
-    lengths = nb_lengths[0]
-    table = jnp.pad(slot_stretch, ((0, 7), (0, 128 - per_dev)))
-    table += jnp.pad(lengths, ((1, 7 - per_dev), (0, 128 - lengths.shape[1])))
     any_spec = pl.BlockSpec(memory_space=pl.ANY)
+    smem_spec = pl.BlockSpec(memory_space=pltpu.SMEM)
     vmem_spec = pl.BlockSpec(memory_space=pltpu.VMEM)
     dma = pltpu.SemaphoreType.DMA
     block = (STRETCH, feats // GROUPS)
     mixed = pl.pallas_call(
         functools.partial(kernel, n_seg, n_seq, n_tp, per_dev),
         out_shape=jax.ShapeDtypeStruct((rows, keep), residual.dtype),
-        in_specs=[any_spec] * 5 + [vmem_spec],
+        in_specs=[any_spec] * 5 + [smem_spec] * 2 + [vmem_spec],
         out_specs=vmem_spec,
         scratch_shapes=[
             pltpu.VMEM((per_dev, span, feats), BF16),
@@ -364,10 +358,10 @@
             pltpu.VMEM((n_tp, per_dev, STRETCH, keep), BF16),
             pltpu.VMEM((n_tp, per_dev, STRETCH, keep), BF16),
             pltpu.VMEM((n_tp, per_dev, STRETCH, keep), BF16),
+            pltpu.VMEM((8, 128), jnp.int32),
             pltpu.VMEM((n_seq, 8, 128), jnp.int32),
             pltpu.SMEM((n_seq, 8, 128), jnp.int32),
-            pltpu.SMEM((8, 128), jnp.int32),
-            dma((6,)),
+            dma((5,)),
             dma((GROUPS,)), dma((GROUPS,)),
             dma((n_seq - 1, GROUPS)), dma((n_seq - 1, GROUPS)),
             dma((GROUPS,)), dma((GROUPS,)),
@@ -382,7 +376,7 @@
         ),
     )(
         queries.reshape(per_dev, STRETCH, feats), nb_keys[0], nb_values[0], out_weight[0],
-        residual[0], table,
+        residual[0], nb_lengths[0].T, slot_stretch, slot_stretch,
     )
     return mixed[None]
 

time: 83.4 us -> 80.9 us (0.970)
  other arithmetic: 1.25 us -> 0 us
    add x1 -> x0, other arithmetic: 1.25 us -> none  [local(): table += jnp.pad(lengths, ((1, 7 - per_dev), (0, 128 - lengths.shape[1])))]
where the time goes in v4:
time: 80.9 us; the launch traced here: 80.7 us
  Pallas kernels  78.9 us (98%)
  local copies, waits for them, and re-layouts  1.77 us (2%)
    pallas_call x1, Pallas kernels, local(): pl.pallas_call(functools.partial(kernel, n_seg, n_seq, n_tp, per_dev), ou...  78.9 us
    unnamed x1, local copies, waits for them, and re-layouts  1.77 us

profile of v4, /device:TPU:2, one launch (start us, length us, event | category | flops | bytes accessed | tf_op | source)
XLA Modules:
  0.0 80.7 jit_solution(5906822537409743757)
XLA Ops:
  0.0 78.9 %shard_map.73 = bf16[192,1024]{1,0:T(8,128)(2,1)} custom-call(bf16[3,64,1024]{2,1,0:T(8,128)(2,1)} %bitcast.13, bf16[3,256,1024]{2,1,0:T(8,128)(2,1)} %bitcast.11, bf16[3,256,1024]{2,1,0:T(8,128)(2,1)} %bitcast.12, bf16[1024,1024]{1,0:T(8,128)(2,1)} %bitcast.9, bf16[192,1024]{1,0:T(8,128)(2,1)} %bitcast.14, s32[2,3]{1,0:T(2,128)} %bitcast.15, ...), custom_call_target="tpu_custom_call" | custom-call | tf_op jit(solution)/shard_map/pallas_call | solution.py:343
  78.9 1.8 %copy.9 = bf16[1,192,1024]{2,1,0:T(8,128)(2,1)} copy(bf16[1,192,1024]{2,1,0:T(8,128)(2,1)} %bitcast.10) | data formatting | bytes 786432

commit v5 on v4

--- a/solution.py
+++ b/solution.py
@@ -12,6 +12,7 @@
 STRETCH = 64
 NR = 128
 GROUPS = 4
+ROWS = 32
 MESH = pl.DeviceIdType.MESH
 F32 = jnp.float32
 BF16 = jnp.bfloat16
@@ -31,7 +32,7 @@
     n_seg, n_seq, n_tp, per_dev,
     q_hbm, k_hbm, v_hbm, w_hbm, res_hbm, len_ref, slot_ref, row_ref,
     out_ref,
-    kbuf, vbuf, wbuf, resbuf, qbufs, abufs, answers, acc, psend, rbuf, upbuf, downbuf, table, tbuf, tsmem,
+    kbuf, vbuf, wbuf, resbuf, qbufs, abufs, answers, psend, rbuf, upbuf, downbuf, table, tbuf, tsmem,
     load_sem, qy_send, qy_recv, qx_send, qx_recv, ay_send, ay_recv, ax_send, ax_recv,
     t_send, t_recv, p_send, p_recv, up_send, up_recv, down_send, down_recv,
 ):
@@ -42,6 +43,7 @@
     feats = q_hbm.shape[2]
     width = w_hbm.shape[1]
     ratio = n_seq // n_tp
+    chunks = per_dev * STRETCH // ROWS
     groups = len(qbufs)
     part = feats // groups
 
@@ -160,26 +162,34 @@
         if g == 0:
             loads[0].wait()
             loads[1].wait()
+        units = [(k, h) for k in range(per_dev) for h in range(part // HD)]
+        wide = [pl.ds(g * part + h * HD, HD) for _, h in units]
+        valid = []
         for k in range(per_dev):
             limit = jnp.zeros((1, span), jnp.int32)
             for j in range(span // NR):
                 inside = (position >= j * NR) & (position < (j + 1) * NR)
                 limit = jnp.where(inside, j * NR + len_ref[j, k], limit)
-            valid = position < limit
-            stretch = slot_ref[0, k]
-            for h in range(part // HD):
-                cols = pl.ds(h * HD, HD)
-                wide = pl.ds(g * part + h * HD, HD)
-                query = qbufs[g][stretch, :, cols]
-                scores = lax.dot_general(
-                    query, kbuf[k, :, wide], (((1,), (1,)), ((), ())), preferred_element_type=F32
-                ) * (1.0 / math.sqrt(HD))
-                scores = jnp.where(valid, scores, -1e30)
-                expo = jnp.exp(scores - jnp.max(scores, axis=1, keepdims=True))
-                weights = (expo * (1.0 / jnp.sum(expo, axis=1, keepdims=True))).astype(BF16)
-                answers[g][k, :, cols] = jnp.dot(
-                    weights, vbuf[k, :, wide], preferred_element_type=F32
-                ).astype(BF16)
+            valid.append(position < limit)
+        scores = [
+            lax.dot_general(
+                qbufs[g][slot_ref[0, k], :, pl.ds(h * HD, HD)], kbuf[k, :, cols],
+                (((1,), (1,)), ((), ())), preferred_element_type=F32,
+            )
+            for (k, h), cols in zip(units, wide)
+        ]
+        scores = [
+            jnp.where(valid[k], one * (1.0 / math.sqrt(HD)), -1e30)
+            for (k, _), one in zip(units, scores)
+        ]
+        highest = [jnp.max(one, axis=1, keepdims=True) for one in scores]
+        expo = [jnp.exp(one - top) for one, top in zip(scores, highest)]
+        sums = [jnp.sum(one, axis=1, keepdims=True) for one in expo]
+        weights = [(one * (1.0 / total)).astype(BF16) for one, total in zip(expo, sums)]
+        for (k, h), cols, one in zip(units, wide, weights):
+            answers[g][k, :, pl.ds(h * HD, HD)] = jnp.dot(
+                one, vbuf[k, :, cols], preferred_element_type=F32
+            ).astype(BF16)
         ay[g].start()
 
     order = list(range(n_seq - 1, -1, -1))
@@ -205,33 +215,29 @@
                     slot = jnp.where(value == partner[m] * per_dev + c, jnp.int32(g), slot)
                 slots[m, c] = slot
 
-    def project(g):
-        if g == 0:
-            find_slots()
-            loads[2].wait()
-        for c in range(per_dev):
-            rows = jnp.concatenate([abufs[g][slots[m, c]] for m in order], axis=0)
+    def project():
+        for k in range(per_dev):
+            rows = [
+                jnp.concatenate([buf[slots[m, k]] for buf in abufs], axis=1) for m in order
+            ]
             product = jnp.dot(
-                rows, wbuf[pl.ds(g * part, part), :], preferred_element_type=F32
-            )
-            if g:
-                product = acc[c] + product
-            if g < groups - 1:
-                acc[c] = product
-                continue
-            product = product.astype(BF16)
-            for at, m in enumerate(order):
-                block = product[at * STRETCH:(at + 1) * STRETCH]
-                if m == 0:
-                    mine(c)[...] = block
-                else:
-                    psend[m - 1, c] = block
-                    copy = remote(
-                        psend.at[m - 1, c], mine(c), p_send.at[m, c], p_recv.at[seq, c],
-                        (seg, partner[m], tp),
-                    )
-                    copy.start()
-                    exchange[m, c] = copy
+                jnp.concatenate(rows, axis=0), wbuf[...], preferred_element_type=F32
+            ).astype(BF16)
+            for piece in range(STRETCH // ROWS):
+                c = k * (STRETCH // ROWS) + piece
+                for at, m in enumerate(order):
+                    start = at * STRETCH + piece * ROWS
+                    block = product[start:start + ROWS]
+                    if m == 0:
+                        mine(c)[...] = block
+                    else:
+                        psend[m - 1, c] = block
+                        copy = remote(
+                            psend.at[m - 1, c], mine(c), p_send.at[m, c], p_recv.at[seq, c],
+                            (seg, partner[m], tp),
+                        )
+                        copy.start()
+                        exchange[m, c] = copy
 
     depth = len(steps)
     stages = [lambda g: enter(qy[g], q_levels[g])]
@@ -239,12 +245,15 @@
     stages[-1] = lambda g: (relay(q_levels[g], depth - 1), attend(g))
     stages += [lambda g: enter(ay[g], a_levels[g])]
     stages += [lambda g, d=d: relay(a_levels[g], d) for d in range(depth)]
-    stages[-1] = lambda g: (relay(a_levels[g], depth - 1), project(g))
     delay = [at + (at > depth) for at in range(len(stages))]
     for turn in range(groups + delay[-1]):
         for stage, late in zip(stages, delay):
             if 0 <= turn - late < groups:
                 stage(turn - late)
+        if turn == groups:
+            find_slots()
+    loads[2].wait()
+    project()
 
     last = n_tp - 1
 
@@ -287,7 +296,7 @@
             @pl.when(tp != end)
             def _():
                 along(buf, send, recv, c, tp, (seg, seq, tp + near)).wait_recv()
-        own = pl.ds(c * STRETCH, STRETCH)
+        own = pl.ds(c * ROWS, ROWS)
         total = upbuf[tp, c].astype(F32) + downbuf[tp, c].astype(F32) + rbuf[tp, c].astype(F32)
         out_ref[own, :] = (resbuf[own, :].astype(F32) + total).astype(out_ref.dtype)
 
@@ -296,8 +305,8 @@
     low = home < near
     targets = [jnp.where(low, p, last - p) for p in range(near)]
     targets += [jnp.where(low, last - p, p) for p in range(near)]
-    visits = [(m, c) for c in range(per_dev) for m in range(near)]
-    visits += [(m, c) for c in range(per_dev) for m in range(near, n_tp)]
+    visits = [(m, c) for c in range(chunks) for m in range(near)]
+    visits += [(m, c) for c in range(chunks) for m in range(near, n_tp)]
     loads[3].wait()
     for m, c in visits:
         target = targets[m]
@@ -311,7 +320,7 @@
         def _():
             push(downbuf, down_send, down_recv, c, target, tp == last, (seg, seq, tp - 1))
 
-    for c in range(per_dev):
+    for c in range(chunks):
         finish(c)
 
     for copy in pending + list(exchange.values()):
@@ -340,6 +349,7 @@
     vmem_spec = pl.BlockSpec(memory_space=pltpu.VMEM)
     dma = pltpu.SemaphoreType.DMA
     block = (STRETCH, feats // GROUPS)
+    chunks = per_dev * STRETCH // ROWS
     mixed = pl.pallas_call(
         functools.partial(kernel, n_seg, n_seq, n_tp, per_dev),
         out_shape=jax.ShapeDtypeStruct((rows, keep), residual.dtype),
@@ -353,11 +363,10 @@
             [pltpu.VMEM((n_seq * per_dev,) + block, BF16)] * GROUPS,
             [pltpu.VMEM((n_seq * per_dev,) + block, BF16)] * GROUPS,
             [pltpu.VMEM((per_dev,) + block, BF16)] * GROUPS,
-            pltpu.VMEM((per_dev, n_seq * STRETCH, width), F32),
-            pltpu.VMEM((n_seq - 1, per_dev, STRETCH, width), BF16),
-            pltpu.VMEM((n_tp, per_dev, STRETCH, keep), BF16),
-            pltpu.VMEM((n_tp, per_dev, STRETCH, keep), BF16),
-            pltpu.VMEM((n_tp, per_dev, STRETCH, keep), BF16),
+            pltpu.VMEM((n_seq - 1, chunks, ROWS, width), BF16),
+            pltpu.VMEM((n_tp, chunks, ROWS, keep), BF16),
+            pltpu.VMEM((n_tp, chunks, ROWS, keep), BF16),
+            pltpu.VMEM((n_tp, chunks, ROWS, keep), BF16),
             pltpu.VMEM((8, 128), jnp.int32),
             pltpu.VMEM((n_seq, 8, 128), jnp.int32),
             pltpu.SMEM((n_seq, 8, 128), jnp.int32),
@@ -367,9 +376,9 @@
             dma((GROUPS,)), dma((GROUPS,)),
             dma((n_seq - 1, GROUPS)), dma((n_seq - 1, GROUPS)),
             dma((n_seq,)), dma((n_seq,)),
-            dma((n_seq, per_dev)), dma((n_seq, per_dev)),
-            dma((n_tp, per_dev)), dma((n_tp, per_dev)),
-            dma((n_tp, per_dev)), dma((n_tp, per_dev)),
+            dma((n_seq, chunks)), dma((n_seq, chunks)),
+            dma((n_tp, chunks)), dma((n_tp, chunks)),
+            dma((n_tp, chunks)), dma((n_tp, chunks)),
         ],
         compiler_params=pltpu.CompilerParams(
             collective_id=0, has_side_effects=True, vmem_limit_bytes=60 * 1024 * 1024

time: 80.9 us -> 79.1 us (0.978)
  Pallas kernels: 78.9 us -> 77.2 us
    pallas_call x1, Pallas kernels: 78.9 us -> 77.2 us  [local(): pl.pallas_call(functools.partial(kernel, n_seg, n_seq, n_tp, per_dev), ou...]
where the time goes in v5:
time: 79.1 us; the launch traced here: 78.9 us
  Pallas kernels  77.2 us (98%)
  local copies, waits for them, and re-layouts  1.77 us (2%)
    pallas_call x1, Pallas kernels, local(): pl.pallas_call(functools.partial(kernel, n_seg, n_seq, n_tp, per_dev), ou...  77.2 us
    unnamed x1, local copies, waits for them, and re-layouts  1.77 us

profile of v5, /device:TPU:2, one launch (start us, length us, event | category | flops | bytes accessed | tf_op | source)
XLA Modules:
  0.0 78.9 jit_solution(12189392590434904413)
XLA Ops:
  0.0 77.2 %shard_map.73 = bf16[192,1024]{1,0:T(8,128)(2,1)} custom-call(bf16[3,64,1024]{2,1,0:T(8,128)(2,1)} %bitcast.13, bf16[3,256,1024]{2,1,0:T(8,128)(2,1)} %bitcast.11, bf16[3,256,1024]{2,1,0:T(8,128)(2,1)} %bitcast.12, bf16[1024,1024]{1,0:T(8,128)(2,1)} %bitcast.9, bf16[192,1024]{1,0:T(8,128)(2,1)} %bitcast.14, s32[2,3]{1,0:T(2,128)} %bitcast.15, ...), custom_call_target="tpu_custom_call" | custom-call | tf_op jit(solution)/shard_map/pallas_call | solution.py:353
  77.2 1.8 %copy.9 = bf16[1,192,1024]{2,1,0:T(8,128)(2,1)} copy(bf16[1,192,1024]{2,1,0:T(8,128)(2,1)} %bitcast.10) | data formatting | bytes 786432

commit v6 on v5

--- a/solution.py
+++ b/solution.py
@@ -13,6 +13,7 @@
 NR = 128
 GROUPS = 4
 ROWS = 32
+AHEAD = 2
 MESH = pl.DeviceIdType.MESH
 F32 = jnp.float32
 BF16 = jnp.bfloat16
@@ -108,7 +109,7 @@
         )
         for g in range(groups)
     ]
-    for copy in qy:
+    for copy in qy[:AHEAD]:
         copy.start()
     pending += qy
 
@@ -215,6 +216,10 @@
                     slot = jnp.where(value == partner[m] * per_dev + c, jnp.int32(g), slot)
                 slots[m, c] = slot
 
+    def send_out(c):
+        for m in range(1, n_seq):
+            exchange[m, c].start()
+
     def project():
         for k in range(per_dev):
             rows = [
@@ -236,11 +241,17 @@
                             psend.at[m - 1, c], mine(c), p_send.at[m, c], p_recv.at[seq, c],
                             (seg, partner[m], tp),
                         )
-                        copy.start()
                         exchange[m, c] = copy
+                if c < AHEAD:
+                    send_out(c)
 
     depth = len(steps)
-    stages = [lambda g: enter(qy[g], q_levels[g])]
+    def enter_queries(g):
+        enter(qy[g], q_levels[g])
+        if g + AHEAD < groups:
+            qy[g + AHEAD].start()
+
+    stages = [enter_queries]
     stages += [lambda g, d=d: relay(q_levels[g], d) for d in range(depth)]
     stages[-1] = lambda g: (relay(q_levels[g], depth - 1), attend(g))
     stages += [lambda g: enter(ay[g], a_levels[g])]
@@ -305,11 +316,15 @@
     low = home < near
     targets = [jnp.where(low, p, last - p) for p in range(near)]
     targets += [jnp.where(low, last - p, p) for p in range(near)]
-    visits = [(m, c) for c in range(chunks) for m in range(near)]
-    visits += [(m, c) for c in range(chunks) for m in range(near, n_tp)]
+    visits = []
+    for step in range(chunks + 1):
+        for at in range(near):
+            visits += [(m, c) for m, c in ((at, step), (near + at, step - 1)) if 0 <= c < chunks]
     loads[3].wait()
     for m, c in visits:
         target = targets[m]
+        if m == 0 and c + AHEAD < chunks:
+            send_out(c + AHEAD)
         arrived(target, c)
 
         @pl.when(target > tp)

time: 79.1 us -> 85.1 us (1.076)
  Pallas kernels: 77.2 us -> 83.2 us
    pallas_call x1, Pallas kernels: 77.2 us -> 83.2 us  [local(): pl.pallas_call(functools.partial(kernel, n_seg, n_seq, n_tp, per_dev), ou...]
where the time goes in v6:
time: 85.1 us; the launch traced here: 84.9 us
  Pallas kernels  83.2 us (98%)
  local copies, waits for them, and re-layouts  1.77 us (2%)
    pallas_call x1, Pallas kernels, local(): pl.pallas_call(functools.partial(kernel, n_seg, n_seq, n_tp, per_dev), ou...  83.2 us
    unnamed x1, local copies, waits for them, and re-layouts  1.77 us

profile of v6, /device:TPU:2, one launch (start us, length us, event | category | flops | bytes accessed | tf_op | source)
XLA Modules:
  0.0 84.9 jit_solution(10032164134751571532)
XLA Ops:
  0.0 83.2 %shard_map.73 = bf16[192,1024]{1,0:T(8,128)(2,1)} custom-call(bf16[3,64,1024]{2,1,0:T(8,128)(2,1)} %bitcast.13, bf16[3,256,1024]{2,1,0:T(8,128)(2,1)} %bitcast.11, bf16[3,256,1024]{2,1,0:T(8,128)(2,1)} %bitcast.12, bf16[1024,1024]{1,0:T(8,128)(2,1)} %bitcast.9, bf16[192,1024]{1,0:T(8,128)(2,1)} %bitcast.14, s32[2,3]{1,0:T(2,128)} %bitcast.15, ...), custom_call_target="tpu_custom_call" | custom-call | tf_op jit(solution)/shard_map/pallas_call | solution.py:368
  83.2 1.8 %copy.9 = bf16[1,192,1024]{2,1,0:T(8,128)(2,1)} copy(bf16[1,192,1024]{2,1,0:T(8,128)(2,1)} %bitcast.10) | data formatting | bytes 786432

commit v7 on v5

--- a/solution.py
+++ b/solution.py
@@ -305,36 +305,50 @@
     low = home < near
     targets = [jnp.where(low, p, last - p) for p in range(near)]
     targets += [jnp.where(low, last - p, p) for p in range(near)]
-    visits = [(m, c) for c in range(chunks) for m in range(near)]
-    visits += [(m, c) for c in range(chunks) for m in range(near, n_tp)]
     loads[3].wait()
-    for m, c in visits:
-        target = targets[m]
+
+    def each(step, rise, fall):
+        for m, target in enumerate(targets):
+            begin = step - m // near
+            up, down = begin - tp, begin - (last - tp)
+
+            @pl.when((target > tp) & (up >= 0) & (up < chunks))
+            def _():
+                rise(target, up)
+
+            @pl.when((target < tp) & (down >= 0) & (down < chunks))
+            def _():
+                fall(target, down)
+
+    def rise(target, c):
         arrived(target, c)
-
-        @pl.when(target > tp)
-        def _():
-            push(upbuf, up_send, up_recv, c, target, tp == 0, (seg, seq, tp + 1))
-
-        @pl.when(target < tp)
-        def _():
-            push(downbuf, down_send, down_recv, c, target, tp == last, (seg, seq, tp - 1))
+        push(upbuf, up_send, up_recv, c, target, tp == 0, (seg, seq, tp + 1))
+
+    def fall(target, c):
+        arrived(target, c)
+        push(downbuf, down_send, down_recv, c, target, tp == last, (seg, seq, tp - 1))
+
+    @pl.loop(0, chunks + 1 + last)
+    def _(step):
+        each(step, rise, fall)
 
     for c in range(chunks):
+        arrived(tp, c)
         finish(c)
 
     for copy in pending + list(exchange.values()):
         copy.wait_send()
-    for m, c in visits:
-        target = targets[m]
-
-        @pl.when(target > tp)
-        def _():
-            along(upbuf, up_send, up_recv, c, target, (seg, seq, tp + 1)).wait_send()
-
-        @pl.when(target < tp)
-        def _():
-            along(downbuf, down_send, down_recv, c, target, (seg, seq, tp - 1)).wait_send()
+    @pl.loop(0, chunks + 1 + last)
+    def _(step):
+        each(
+            step,
+            lambda target, c: along(
+                upbuf, up_send, up_recv, c, target, (seg, seq, tp + 1)
+            ).wait_send(),
+            lambda target, c: along(
+                downbuf, down_send, down_recv, c, target, (seg, seq, tp - 1)
+            ).wait_send(),
+        )
 
 
 def local(sizes, queries, nb_keys, nb_values, nb_lengths, slot_stretch, out_weight, residual):

time: 79.1 us -> 71.6 us (0.905)
  Pallas kernels: 77.2 us -> 69.7 us
    pallas_call x1, Pallas kernels: 77.2 us -> 69.7 us  [local(): pl.pallas_call(functools.partial(kernel, n_seg, n_seq, n_tp, per_dev), ou...]
where the time goes in v7:
time: 71.6 us; the launch traced here: 71.5 us
  Pallas kernels  69.7 us (97%)
  local copies, waits for them, and re-layouts  1.77 us (2%)
    pallas_call x1, Pallas kernels, local(): pl.pallas_call(functools.partial(kernel, n_seg, n_seq, n_tp, per_dev), ou...  69.7 us
    unnamed x1, local copies, waits for them, and re-layouts  1.77 us

profile of v7, /device:TPU:2, one launch (start us, length us, event | category | flops | bytes accessed | tf_op | source)
XLA Modules:
  0.0 71.5 jit_solution(6453805084925248615)
XLA Ops:
  0.0 69.7 %shard_map.73 = bf16[192,1024]{1,0:T(8,128)(2,1)} custom-call(bf16[3,64,1024]{2,1,0:T(8,128)(2,1)} %bitcast.13, bf16[3,256,1024]{2,1,0:T(8,128)(2,1)} %bitcast.11, bf16[3,256,1024]{2,1,0:T(8,128)(2,1)} %bitcast.12, bf16[1024,1024]{1,0:T(8,128)(2,1)} %bitcast.9, bf16[192,1024]{1,0:T(8,128)(2,1)} %bitcast.14, s32[2,3]{1,0:T(2,128)} %bitcast.15, ...), custom_call_target="tpu_custom_call" | custom-call | tf_op jit(solution)/shard_map/pallas_call | solution.py:367
  69.7 1.8 %copy.9 = bf16[1,192,1024]{2,1,0:T(8,128)(2,1)} copy(bf16[1,192,1024]{2,1,0:T(8,128)(2,1)} %bitcast.10) | data formatting | bytes 786432

commit v8 on v7

--- a/solution.py
+++ b/solution.py
@@ -13,6 +13,7 @@
 NR = 128
 GROUPS = 4
 ROWS = 32
+AHEAD = 2
 MESH = pl.DeviceIdType.MESH
 F32 = jnp.float32
 BF16 = jnp.bfloat16
@@ -108,7 +109,7 @@
         )
         for g in range(groups)
     ]
-    for copy in qy:
+    for copy in qy[:AHEAD]:
         copy.start()
     pending += qy
 
@@ -240,7 +241,12 @@
                         exchange[m, c] = copy
 
     depth = len(steps)
-    stages = [lambda g: enter(qy[g], q_levels[g])]
+    def enter_queries(g):
+        enter(qy[g], q_levels[g])
+        if g + AHEAD < groups:
+            qy[g + AHEAD].start()
+
+    stages = [enter_queries]
     stages += [lambda g, d=d: relay(q_levels[g], d) for d in range(depth)]
     stages[-1] = lambda g: (relay(q_levels[g], depth - 1), attend(g))
     stages += [lambda g: enter(ay[g], a_levels[g])]
@@ -296,7 +302,7 @@
             @pl.when(tp != end)
             def _():
                 along(buf, send, recv, c, tp, (seg, seq, tp + near)).wait_recv()
-        own = pl.ds(c * ROWS, ROWS)
+        own = pl.ds(pl.multiple_of(c * ROWS, ROWS), ROWS)
         total = upbuf[tp, c].astype(F32) + downbuf[tp, c].astype(F32) + rbuf[tp, c].astype(F32)
         out_ref[own, :] = (resbuf[own, :].astype(F32) + total).astype(out_ref.dtype)
 
@@ -331,10 +337,13 @@
     @pl.loop(0, chunks + 1 + last)
     def _(step):
         each(step, rise, fall)
-
-    for c in range(chunks):
-        arrived(tp, c)
-        finish(c)
+        late = jnp.where(low == (tp < near), 0, 1)
+        c = step - jnp.maximum(tp, last - tp) - late
+
+        @pl.when((c >= 0) & (c < chunks))
+        def _():
+            arrived(tp, c)
+            finish(c)
 
     for copy in pending + list(exchange.values()):
         copy.wait_send()

time: 71.6 us -> 71.9 us (level)
  no operation moved by 1% of the time
where the time goes in v8:
time: 71.9 us; the launch traced here: 71.7 us
  Pallas kernels  70 us (97%)
  local copies, waits for them, and re-layouts  1.77 us (2%)
    pallas_call x1, Pallas kernels, local(): pl.pallas_call(functools.partial(kernel, n_seg, n_seq, n_tp, per_dev), ou...  70 us
    unnamed x1, local copies, waits for them, and re-layouts  1.77 us

profile of v8, /device:TPU:2, one launch (start us, length us, event | category | flops | bytes accessed | tf_op | source)
XLA Modules:
  0.0 71.7 jit_solution(1988917140334727528)
XLA Ops:
  0.0 70.0 %shard_map.73 = bf16[192,1024]{1,0:T(8,128)(2,1)} custom-call(bf16[3,64,1024]{2,1,0:T(8,128)(2,1)} %bitcast.13, bf16[3,256,1024]{2,1,0:T(8,128)(2,1)} %bitcast.11, bf16[3,256,1024]{2,1,0:T(8,128)(2,1)} %bitcast.12, bf16[1024,1024]{1,0:T(8,128)(2,1)} %bitcast.9, bf16[192,1024]{1,0:T(8,128)(2,1)} %bitcast.14, s32[2,3]{1,0:T(2,128)} %bitcast.15, ...), custom_call_target="tpu_custom_call" | custom-call | tf_op jit(solution)/shard_map/pallas_call | solution.py:376
  70.0 1.8 %copy.9 = bf16[1,192,1024]{2,1,0:T(8,128)(2,1)} copy(bf16[1,192,1024]{2,1,0:T(8,128)(2,1)} %bitcast.10) | data formatting | bytes 786432

commit v9 on v8

--- a/solution.py
+++ b/solution.py
@@ -12,8 +12,8 @@
 STRETCH = 64
 NR = 128
 GROUPS = 4
-ROWS = 32
-AHEAD = 2
+ROWS = 16
+AHEAD = GROUPS
 MESH = pl.DeviceIdType.MESH
 F32 = jnp.float32
 BF16 = jnp.bfloat16

time: 71.9 us -> 76.7 us (1.067)
  Pallas kernels: 70 us -> 74.7 us
    pallas_call x1, Pallas kernels: 70 us -> 74.7 us  [local(): pl.pallas_call(functools.partial(kernel, n_seg, n_seq, n_tp, per_dev), ou...]
where the time goes in v9:
time: 76.7 us; the launch traced here: 76.5 us
  Pallas kernels  74.7 us (97%)
  local copies, waits for them, and re-layouts  1.77 us (2%)
    pallas_call x1, Pallas kernels, local(): pl.pallas_call(functools.partial(kernel, n_seg, n_seq, n_tp, per_dev), ou...  74.7 us
    unnamed x1, local copies, waits for them, and re-layouts  1.77 us

profile of v9, /device:TPU:2, one launch (start us, length us, event | category | flops | bytes accessed | tf_op | source)
XLA Modules:
  0.0 76.5 jit_solution(16167148196128732474)
XLA Ops:
  0.0 74.7 %shard_map.73 = bf16[192,1024]{1,0:T(8,128)(2,1)} custom-call(bf16[3,64,1024]{2,1,0:T(8,128)(2,1)} %bitcast.13, bf16[3,256,1024]{2,1,0:T(8,128)(2,1)} %bitcast.11, bf16[3,256,1024]{2,1,0:T(8,128)(2,1)} %bitcast.12, bf16[1024,1024]{1,0:T(8,128)(2,1)} %bitcast.9, bf16[192,1024]{1,0:T(8,128)(2,1)} %bitcast.14, s32[2,3]{1,0:T(2,128)} %bitcast.15, ...), custom_call_target="tpu_custom_call" | custom-call | tf_op jit(solution)/shard_map/pallas_call | solution.py:376
  74.7 1.8 %copy.9 = bf16[1,192,1024]{2,1,0:T(8,128)(2,1)} copy(bf16[1,192,1024]{2,1,0:T(8,128)(2,1)} %bitcast.10) | data formatting | bytes 786432
